TPU v7x, 512 devices: a whole 4x4x16 slice. The times are simulated.
512 devices in a mesh: batch: 64 (over z, x_hi, core), tensor: 8 (over y, x_lo).
Axes of the slice: x: 4 (x_hi: 2, x_lo: 2; x = x_hi * 2 + x_lo), y: 4, z: 16, core: 2. Of those that a mesh axis runs over, the one named last changes fastest.
Arguments:
- stream: float32 [512, 4096], P('batch', 'tensor'), may hold values from -60 to 60
- code_ids: int32 [512, 2, 32], P('batch'), may hold values from 0 to 2047
- back_gain: float32 [4096], P('tensor'), may hold values from 0.5 to 1.5
- projection: bfloat16 [4096, 1024], P('tensor'), may hold values from -0.09375 to 0.09375
- code_table: bfloat16 [32, 2048, 4096], P(None, 'tensor', 'batch'), may hold values from -2.7 to 2.7
- depth_table: bfloat16 [31, 2048, 1024], P(None, 'tensor', 'batch'), may hold values from -8 to 8
- depth_gain: float32 [1, 1024], replicated, may hold values from 0.5 to 1.5
- qkv_weight: bfloat16 [1, 1024, 3, 1024], P(None, None, None, 'tensor'), may hold values from -0.15625 to 0.15625
- out_weight: bfloat16 [1, 1024, 1024], P(None, 'tensor'), may hold values from -0.1875 to 0.1875
Outputs:
- depth_states: bfloat16 [2, 512, 32, 1024], P(None, 'batch', None, 'tensor')
- next_stream: float32 [512, 4096], P('batch', 'tensor')
Inputs may be any that keep to these rules, and one draw needn't show every extreme that they name: `code_ids`: each id is below 2048; ids may cross devices in any lossless form, several packed to a word.
All inputs are finite; a program needn't handle non-finite values.
Results may differ from a plain program's by a relative error of at most 0.0063.
Values may be sent and summed in bfloat16 or wider, within the bound.
A program may use at most 64 MiB of HBM per device.

v0:
```python
import jax
import jax.numpy as jnp
from jax import lax
from jax.sharding import PartitionSpec as P

D = 4096
HD = 128


epsilon = 1e-05


def rms_norm(values_in, gain):
    return (
        values_in
        * lax.rsqrt(jnp.mean(values_in * values_in, axis=-1, keepdims=True) + epsilon)
        * gain
    )


def attend(normed, qkv_layer, out_layer):
    row_count, positions, _ = normed.shape
    width_here = qkv_layer.shape[2]
    head_count = width_here // HD
    packed = jnp.einsum(
        "rpd,dch->rpch", normed, qkv_layer, preferred_element_type=jnp.float32
    ).astype(jnp.bfloat16)
    query_part = packed[:, :, 0].reshape(row_count, positions, head_count, HD)
    key_part = packed[:, :, 1].reshape(row_count, positions, head_count, HD)
    value_part = packed[:, :, 2].reshape(row_count, positions, head_count, HD)
    scores = jnp.einsum(
        "rphe,rqhe->rhpq", query_part, key_part, preferred_element_type=jnp.float32
    ) * HD ** (-0.5)
    causal = lax.broadcasted_iota(jnp.int32, (positions, positions), 0) >= lax.broadcasted_iota(
        jnp.int32, (positions, positions), 1
    )
    scores = jnp.where(causal, scores, -1e30)
    scores = scores - jnp.max(scores, axis=-1, keepdims=True)
    weights = jnp.exp(scores)
    probs_low = (weights / jnp.sum(weights, axis=-1, keepdims=True)).astype(jnp.bfloat16)
    blended = jnp.einsum(
        "rhpq,rqhe->rphe", probs_low, value_part, preferred_element_type=jnp.float32
    )
    blended = blended.astype(jnp.bfloat16).reshape(row_count, positions, width_here)
    return jnp.einsum("rph,hd->rpd", blended, out_layer, preferred_element_type=jnp.float32)


def frame_hidden(stream, back_gain):
    square_sum = lax.psum(jnp.sum(stream * stream, axis=1), "tensor")
    return (stream * lax.rsqrt(square_sum / D + epsilon)[:, None] * back_gain).astype(jnp.bfloat16)


def on_device(
    stream,
    code_ids,
    back_gain,
    projection,
    code_table,
    depth_table,
    depth_gain,
    qkv_weight,
    out_weight,
):
    frame_count = code_ids.shape[1]
    book_count = code_ids.shape[2]
    tensor_pos = lax.axis_index("tensor")
    vocab_local = code_table.shape[1]
    vocab_start = tensor_pos * vocab_local
    every_code = lax.all_gather(code_ids, "batch", axis=0, tiled=True)
    code_terms = []
    depth_terms = []
    for frame_idx in range(frame_count):
        shifted = every_code[:, frame_idx, :] - vocab_start
        one_hot = (
            shifted[:, :, None] == lax.broadcasted_iota(jnp.int32, (1, 1, vocab_local), 2)
        ).astype(jnp.bfloat16)
        code_terms.append(
            jnp.einsum("rkv,kvd->rd", one_hot, code_table, preferred_element_type=jnp.float32)
        )
        depth_terms.append(
            jnp.einsum(
                "rkv,kvc->rkc",
                one_hot[:, : book_count - 1],
                depth_table,
                preferred_element_type=jnp.float32,
            ).astype(jnp.bfloat16)
        )
    code_sums = jnp.stack(code_terms, axis=1)
    code_features = lax.all_to_all(
        jnp.stack(depth_terms, axis=1), "batch", split_axis=0, concat_axis=3, tiled=True
    )
    moved_sums = lax.all_to_all(code_sums, "batch", split_axis=0, concat_axis=2, tiled=True)
    summed = lax.psum_scatter(moved_sums, "tensor", scatter_dimension=2, tiled=True)
    results = []
    looked = lax.psum_scatter(
        code_features.astype(jnp.float32).astype(jnp.bfloat16),
        "tensor",
        scatter_dimension=3,
        tiled=True,
    ).astype(jnp.float32)
    for frame_idx in range(frame_count):
        hidden = frame_hidden(stream, back_gain)
        leading = lax.psum_scatter(
            jnp.dot(hidden, projection, preferred_element_type=jnp.float32),
            "tensor",
            scatter_dimension=1,
            tiled=True,
        )
        residual = jnp.concatenate([leading[:, None, :], looked[:, frame_idx]], axis=1)
        full_width = lax.all_gather(residual, "tensor", axis=2, tiled=True)
        normed = rms_norm(full_width, depth_gain[0]).astype(jnp.bfloat16)
        partial_out = attend(normed, qkv_weight[0], out_weight[0])
        residual = residual + lax.psum_scatter(
            partial_out, "tensor", scatter_dimension=2, tiled=True
        )
        results.append(residual.astype(jnp.bfloat16))
        stream = stream + summed[:, frame_idx]
    states = jnp.stack(results)
    return (states, stream)


def solution(mesh):
    return jax.shard_map(
        on_device,
        mesh=mesh,
        in_specs=(
            P("batch", "tensor"),
            P("batch", None, None),
            P("tensor"),
            P("tensor", None),
            P(None, "tensor", "batch"),
            P(None, "tensor", "batch"),
            P(),
            P(None, None, None, "tensor"),
            P(None, "tensor", None),
        ),
        out_specs=(P(None, "batch", None, "tensor"), P("batch", "tensor")),
        check_vma=False,
    )
```

profile of v0, /device:TPU:1, one launch (start us, length us, event | category | flops | bytes accessed | tf_op | source)
XLA Modules:
  0.0 570.4 jit_solution(11249772165435316990)
XLA Ops:
  7.2 86.4 %all_gather.9 = s32[512,2,32]{2,1,0:T(2,128)S(1)} all-gather(s32[8,2,32]{2,1,0:T(2,128)} %param.10), channel_id=1, replica_groups=mesh['batch'=64,'tensor'=8] {'batch'}, dimensions={0}, use_global_device_ids=true | all-gather | bytes 133120 | tf_op jit(solution)/shard_map/all_gather | solution.py:69
  94.2 3.4 fusion.17
  97.6 3.4 fusion.16
  102.6 6.8 %all-to-all-start.1 = ((f32[64,1,1024]{2,1,0:T(1,128)}), f32[64,1,1024]{2,1,0:T(1,128)S(1)}, u32[]{:S(2)}, u32[]{:S(2)}) async-start(f32[64,1,1024]{2,1,0:T(1,128)} %reshape.122), calls=%async_computation.3 | async-start | bytes 524288 | tf_op jit(solution)/shard_map/all_to_all | solution.py:92
  109.4 3.4 fusion.13
  112.8 3.4 fusion.12
  116.3 7.4 %copy.51 = bf16[512,2,31,16]{2,3,1,0:T(8,128)(2,1)} copy(bf16[512,2,31,16]{0,3,2,1:T(8,128)(2,1)S(1)} %pad_maximum_fusion) | data formatting | bytes 2031616 | tf_op jit(solution)/shard_map/stack | solution.py:90
  123.7 9.0 %reshape.120 = bf16[64,2,3968]{2,1,0:T(2,128)(2,1)} reshape(bf16[512,2,16,31]{3,2,1,0:T(8,128)(2,1)} %bitcast.134) | data formatting | bytes 2031616
  133.2 14.7 %all-to-all-start = ((bf16[64,2,3968]{2,1,0:T(2,128)(2,1)}), bf16[64,2,3968]{2,1,0:T(2,128)(2,1)S(1)}, u32[]{:S(2)}, u32[]{:S(2)}) async-start(bf16[64,2,3968]{2,1,0:T(2,128)(2,1)} %reshape.120), calls=%async_computation.1 | async-start | bytes 2031616 | tf_op jit(solution)/shard_map/all_to_all | solution.py:89
  151.3 49.5 %all-to-all-done = bf16[64,2,3968]{2,1,0:T(2,128)(2,1)S(1)} async-done(((bf16[64,2,3968]{2,1,0:T(2,128)(2,1)}), bf16[64,2,3968]{2,1,0:T(2,128)(2,1)S(1)}, u32[]{:S(2)}, u32[]{:S(2)}) %all-to-all-start) | async-done | bytes 1015840 | tf_op jit(solution)/shard_map/all_to_all | solution.py:89
  200.8 11.9 %reshape.121 = bf16[512,2,16,31]{3,2,1,0:T(8,128)(2,1)} reshape(bf16[64,2,3968]{2,1,0:T(2,128)(2,1)S(1)} %all-to-all-done) | data formatting | bytes 2031616
  212.7 3.3 copy.52
  215.9 4.6 copy.69
  220.6 7.0 %reshape.118 = bf16[1024,496]{1,0:T(8,128)(2,1)} reshape(bf16[1024,2,8,31]{3,2,1,0:T(8,128)(2,1)} %bitcast.136) | data formatting | bytes 2031616
  227.7 1.5 multiply_reduce_fusion.3
  229.3 16.9 %all-reduce = (f32[8]{0:T(128)S(1)}, f32[8]{0:T(128)S(1)}) all-reduce(f32[8]{0:T(128)S(1)} %get-tuple-element.3, f32[8]{0:T(128)S(1)} %get-tuple-element.2), channel_id=1, replica_groups=mesh['batch'=64,'tensor'=8] {'tensor'}, use_global_device_ids=true, to_apply=%region_10.11 | all-reduce | flops 16 | bytes 128 | tf_op jit(solution)/shard_map/psum | solution.py:49
  246.2 1.7 fusion.47
  248.9 16.1 %reduce-scatter.19.cloned.1.call-done = bf16[128,496]{1,0:T(8,128)(2,1)} async-done(((bf16[1024,496]{1,0:T(8,128)(2,1)}), bf16[128,496]{1,0:T(8,128)(2,1)}) %reduce-scatter.19.cloned.1.call-update) | async-done | bytes 126992
  265.1 1.6 reshape.119
  267.2 44.3 %reduce-scatter.15.cloned.1.call-done = f32[8,128]{1,0:T(8,128)} async-done(((f32[8,1024]{1,0:T(8,128)}), f32[8,128]{1,0:T(8,128)}) %reduce-scatter.15.cloned.1.call-update) | async-done | bytes 4112 | tf_op jit(solution)/shard_map/reduce_scatter | solution.py:103
  313.0 44.3 %reduce-scatter.9.cloned.1.call-done = f32[8,128]{1,0:T(8,128)} async-done(((f32[8,1024]{1,0:T(8,128)}), f32[8,128]{1,0:T(8,128)}) %reduce-scatter.9.cloned.1.call-update) | async-done | bytes 4112 | tf_op jit(solution)/shard_map/reduce_scatter | solution.py:103
  357.3 1.3 pad_maximum_fusion.2
  358.8 48.7 %all-gather.5.cloned.1.call-done = f32[8,32,1024]{2,1,0:T(8,128)} async-done(((f32[8,32,128]{2,1,0:T(8,128)}), f32[8,32,1024]{2,1,0:T(8,128)}) %all-gather.5.cloned.1.call-update) | async-done | bytes 1048592 | tf_op jit(solution)/shard_map/all_gather | solution.py:110
  407.4 1.4 multiply_reduce_fusion
  408.8 1.7 convolution_convert_fusion
  410.8 1.5 fusion.24
  412.3 46.1 %all-gather.3.cloned.1.call-done = f32[8,32,1024]{2,1,0:T(8,128)} async-done(((f32[8,32,128]{2,1,0:T(8,128)}), f32[8,32,1024]{2,1,0:T(8,128)}) %all-gather.3.cloned.1.call-update) | async-done | bytes 1048592 | tf_op jit(solution)/shard_map/all_gather | solution.py:110
  458.5 1.4 multiply_reduce_fusion.1
  459.8 1.7 convolution_convert_fusion.1
  461.8 1.5 fusion.25
  463.3 48.0 %reduce-scatter.17.cloned.1.call-done = f32[8,32,128]{2,1,0:T(8,128)} async-done(((f32[8,32,1024]{2,1,0:T(8,128)}), f32[8,32,128]{2,1,0:T(8,128)}) %reduce-scatter.17.cloned.1.call-update) | async-done | bytes 131088 | tf_op jit(solution)/shard_map/reduce_scatter | solution.py:113
  512.2 49.8 %reduce-scatter.11.cloned.1.call-done = f32[8,32,128]{2,1,0:T(8,128)} async-done(((f32[8,32,1024]{2,1,0:T(8,128)}), f32[8,32,128]{2,1,0:T(8,128)}) %reduce-scatter.11.cloned.1.call-update) | async-done | bytes 131088 | tf_op jit(solution)/shard_map/reduce_scatter | solution.py:113
  (68 shorter events, 12.2 us)
Async XLA Ops:
  7.2 87.0 %copy-start = (bf16[32,256,64]{1,2,0:T(8,128)(2,1)S(1)}, bf16[32,256,64]{1,2,0:T(8,128)(2,1)}, u32[]{:S(2)}) copy-start(bf16[32,256,64]{1,2,0:T(8,128)(2,1)} %param.13) | copy-start | bytes 3145732
  97.6 11.8 %copy-start.9 = (bf16[31,256,16]{1,2,0:T(8,128)(2,1)S(1)}, bf16[31,256,16]{1,2,0:T(8,128)(2,1)}, u32[]{:S(2)}) copy-start(bf16[31,256,16]{1,2,0:T(8,128)(2,1)} %param.14) | copy-start | bytes 761860
  102.6 30.6 %all-to-all-start.1 = ((f32[64,1,1024]{2,1,0:T(1,128)}), f32[64,1,1024]{2,1,0:T(1,128)S(1)}, u32[]{:S(2)}, u32[]{:S(2)}) async-start(f32[64,1,1024]{2,1,0:T(1,128)} %reshape.122), calls=%async_computation.3 | async-start | bytes 524288 | tf_op jit(solution)/shard_map/all_to_all | solution.py:92
  133.2 67.6 %all-to-all-start = ((bf16[64,2,3968]{2,1,0:T(2,128)(2,1)}), bf16[64,2,3968]{2,1,0:T(2,128)(2,1)S(1)}, u32[]{:S(2)}, u32[]{:S(2)}) async-start(bf16[64,2,3968]{2,1,0:T(2,128)(2,1)} %reshape.120), calls=%async_computation.1 | async-start | bytes 2031616 | tf_op jit(solution)/shard_map/all_to_all | solution.py:89
  147.9 79.8 %reduce-scatter.13.cloned.1.call-start = ((), (), s32[]{:S(2)}) async-start(), calls=%async_computation.11 | async-start | bytes 294912 | tf_op jit(solution)/shard_map/reduce_scatter | solution.py:93
  151.2 113.8 %reduce-scatter.19.cloned.1.call-start = ((), (), s32[]{:S(2)}) async-start(), calls=%async_computation.15 | async-start | bytes 1179648
  220.6 7.1 %copy-start.4 = (f32[8,512]{1,0:T(8,128)S(1)}, f32[8,512]{1,0:T(8,128)}, u32[]{:S(2)}) copy-start(f32[8,512]{1,0:T(8,128)} %param.9) | copy-start | bytes 49156
  220.6 25.6 %copy-start.1 = (bf16[512,1024]{1,0:T(8,128)(2,1)S(1)}, bf16[512,1024]{1,0:T(8,128)(2,1)}, u32[]{:S(2)}) copy-start(bf16[512,1024]{1,0:T(8,128)(2,1)} %param.12) | copy-start | bytes 3145732
  220.6 25.6 %copy-start.8 = (f32[512]{0:T(512)S(1)}, f32[512]{0:T(512)}, u32[]{:S(2)}) copy-start(f32[512]{0:T(512)} %param.11) | copy-start | bytes 6148
  227.6 181.2 %copy-start.2 = (bf16[1,1024,3,128]{3,1,2,0:T(8,128)(2,1)S(1)}, bf16[1,1024,3,128]{3,1,2,0:T(8,128)(2,1)}, u32[]{:S(2)}) copy-start(bf16[1,1024,3,128]{3,1,2,0:T(8,128)(2,1)} %param.16) | copy-start | bytes 2359300
  227.6 181.2 %copy-start.5 = (f32[1,1024]{1,0:T(1,128)S(1)}, f32[1,1024]{1,0:T(1,128)}, u32[]{:S(2)}) copy-start(f32[1,1024]{1,0:T(1,128)} %param.15) | copy-start | bytes 12292
  227.6 84.0 %reduce-scatter.15.cloned.1.call-start = ((), (), s32[]{:S(2)}) async-start(), calls=%async_computation.12 | async-start | bytes 36864 | tf_op jit(solution)/shard_map/reduce_scatter | solution.py:103
  246.2 164.5 %copy-start.3 = (bf16[1,128,1024]{2,1,0:T(8,128)(2,1)S(1)}, bf16[1,128,1024]{2,1,0:T(8,128)(2,1)}, u32[]{:S(2)}) copy-start(bf16[1,128,1024]{2,1,0:T(8,128)(2,1)} %param.17) | copy-start | bytes 786436
  247.9 109.4 %reduce-scatter.9.cloned.1.call-start = ((), (), s32[]{:S(2)}) async-start(), calls=%async_computation.8 | async-start | bytes 36864 | tf_op jit(solution)/shard_map/reduce_scatter | solution.py:103
  248.9 158.5 %all-gather.5.cloned.1.call-start = ((), (), s32[]{:S(2)}) async-start(), calls=%async_computation.13 | async-start | bytes 1179648 | tf_op jit(solution)/shard_map/all_gather | solution.py:110
  312.9 145.5 %all-gather.3.cloned.1.call-start = ((), (), s32[]{:S(2)}) async-start(), calls=%async_computation.9 | async-start | bytes 1179648 | tf_op jit(solution)/shard_map/all_gather | solution.py:110
  358.7 152.6 %reduce-scatter.17.cloned.1.call-start = ((), (), s32[]{:S(2)}) async-start(), calls=%async_computation.14 | async-start | bytes 1179648 | tf_op jit(solution)/shard_map/reduce_scatter | solution.py:113
  410.8 100.5 %copy-start.6 = (f32[8,128]{1,0:T(8,128)S(1)}, f32[8,128]{1,0:T(8,128)}, u32[]{:S(2)}) copy-start(f32[8,128]{1,0:T(8,128)} %reduce-scatter.15.cloned.1.call-done) | copy-start | bytes 12292
  410.8 151.2 %copy-start.7 = (f32[8,128]{1,0:T(8,128)S(1)}, f32[8,128]{1,0:T(8,128)}, u32[]{:S(2)}) copy-start(f32[8,128]{1,0:T(8,128)} %reduce-scatter.9.cloned.1.call-done) | copy-start | bytes 12292
  412.3 149.7 %reduce-scatter.11.cloned.1.call-start = ((), (), s32[]{:S(2)}) async-start(), calls=%async_computation.10 | async-start | bytes 1179648 | tf_op jit(solution)/shard_map/reduce_scatter | solution.py:113
Sparse Core Ops, SparseCore 0:
  151.6 42.2 reduce-scatter.12
  227.8 37.2 reduce-scatter.18
  268.7 42.8 reduce-scatter.14
  314.2 43.0 reduce-scatter.8
  360.0 47.4 all-gather.4
  409.5 48.9 all-gather.2
  461.5 49.7 reduce-scatter.16
  514.3 47.6 reduce-scatter.10
where the time goes:
time: 575 us; the launch traced here: 570 us
  waiting for transfers between devices  348 us (61%)
  blocking collectives  103 us (18%)
  local copies, waits for them, and re-layouts  49 us (9%)
  matrix products  22.8 us (4%)
  starting transfers between devices  21.9 us (4%)
  between operations  14.4 us (3%)
  other arithmetic  11.4 us (2%)
    reduce_scatter x2, waiting for transfers between devices, on_device(): lax.psum_scatter(partial_out, 'tensor', scatter_dimension=2, tiled=True)  97.7 us
    all_gather x2, waiting for transfers between devices, on_device(): full_width = lax.all_gather(residual, 'tensor', axis=2, tiled=True)  94.8 us
    reduce_scatter x2, waiting for transfers between devices, on_device(): lax.psum_scatter(jnp.dot(hidden, projection, preferred_element_type=jnp.f...  88.7 us
    all_gather x1, blocking collectives, on_device(): every_code = lax.all_gather(code_ids, 'batch', axis=0, tiled=True)  86.4 us
    all_to_all x1, waiting for transfers between devices, on_device(): lax.all_to_all(jnp.stack(depth_terms, axis=1), 'batch', split_axis=0, con...  49.5 us
    unnamed x28, local copies, waits for them, and re-layouts  36.3 us
    psum x1, blocking collectives, frame_hidden(): square_sum = lax.psum(jnp.sum(stream * stream, axis=1), 'tensor')  16.9 us
    unnamed x9, waiting for transfers between devices  16.3 us
  transfers between devices with their start and end apart: 10, of which 9 were waited for; matrix products, arithmetic and copies ran while one was open for 13% of the time, Pallas kernels for 0%

commit v1 on v0

v1 whole, which is shorter than its diff:
```python
import jax
import jax.numpy as jnp
from jax import lax
from jax.experimental import pallas as pl
from jax.experimental.pallas import tpu as pltpu
from jax.sharding import PartitionSpec as P

D = 4096
DD = 1024
HD = 128
NC = 32
VL = 256
EPS = 1e-05
MESH = pl.DeviceIdType.MESH
F32 = jnp.float32
BF16 = jnp.bfloat16


def lane_iota(shape):
    return lax.broadcasted_iota(jnp.int32, shape, len(shape) - 1)


def kernel(
    stream_h, ids_h, bgain_h, proj_h, code_h, depth_h, dgain_h, qkv_h, wo_h,
    states_o, next_o,
    ids_v, stream_v, bgain_v, proj_v, code_v, dgain_v, wq, wo,
    g_ids, e_ids, idt, tb, dsum, sb, rb, zb, xf, nx, lb, ld,
    cb, cr, cs_src, cs, bs, bl, osum,
    loc, snd, rcv,
):
    b = lax.axis_index("batch")
    t = lax.axis_index("tensor")
    z = b // 4
    g = b % 4
    core = b % 2
    chip = b // 2
    mine = 2 * t + core

    def local(src, dst, sem):
        copy = pltpu.make_async_copy(src, dst, sem)
        copy.start()
        return copy

    def remote(src, dst, send_sem, recv_sem, to_b, to_t):
        pltpu.make_async_remote_copy(
            src_ref=src, dst_ref=dst, send_sem=send_sem, recv_sem=recv_sem,
            device_id=(to_b, to_t), device_id_type=MESH,
        ).start()

    def drain(ref, sem):
        pltpu.make_async_copy(ref, ref, sem).wait()

    ids_copy = local(ids_h, ids_v, loc.at[0])
    stream_copy = local(stream_h, stream_v, loc.at[1])
    bgain_copy = local(bgain_h, bgain_v, loc.at[2])
    proj_copy = local(proj_h, proj_v, loc.at[3])

    barrier = pltpu.get_barrier_semaphore()
    for step in range(1, 16):
        pl.semaphore_signal(barrier, inc=1, device_id=((z + step) % 16 * 4 + g, t), device_id_type=MESH)
    for step in range(1, 4):
        pl.semaphore_signal(barrier, inc=1, device_id=(z * 4 + (g + step) % 4, t), device_id_type=MESH)
    for step in range(1, 8):
        for side in range(2):
            pl.semaphore_signal(barrier, inc=1, device_id=(chip * 2 + side, (t + step) % 8), device_id_type=MESH)

    code_copy = local(code_h, code_v, loc.at[4])
    dgain_copy = local(dgain_h, dgain_v, loc.at[5])
    for part in range(3):
        local(qkv_h.at[part], wq.at[:, pl.ds(part * HD, HD)], loc.at[6])

    ids_copy.wait()
    slot = g * 16 + z
    packed = ids_v[:, 0, :] * 2048 + ids_v[:, 1, :]
    g_ids[slot] = jnp.concatenate([packed[r : r + 1, :] for r in range(8)], axis=1)

    pl.semaphore_wait(barrier, 32)

    for step in range(1, 16):
        remote(g_ids.at[slot], g_ids.at[slot], snd.at[0], rcv.at[0], (z + step) % 16 * 4 + g, t)
    for step in range(16):
        to = (mine + step) % 16
        first = jnp.maximum(2 * to - 1, 0)
        src = depth_h.at[pl.ds(first, 2)]
        dst = tb.at[:, pl.ds(pl.multiple_of(core * 16, 16), 16), pl.ds(pl.multiple_of(t * VL, VL), VL)]
        if step == 0:
            local(src, dst, rcv.at[2])
        else:
            remote(src, dst, snd.at[2], rcv.at[2], chip * 2 + to % 2, to // 2)

    def send_leading(frame, current):
        scaled = (current * bgain_v[...]).astype(BF16)
        lb[frame, t, :, 0:DD] = jnp.dot(scaled, proj_v[...], preferred_element_type=F32)
        square = jnp.sum(current * current, axis=1, keepdims=True)
        lb[frame, t, :, DD : DD + 128] = jnp.broadcast_to(square, (8, 128))
        for step in range(1, 8):
            remote(lb.at[frame, t], lb.at[frame, t], snd.at[3 + frame], rcv.at[3 + frame], b, (t + step) % 8)

    stream_copy.wait()
    bgain_copy.wait()
    proj_copy.wait()
    send_leading(0, stream_v[...])

    drain(g_ids.at[pl.ds(0, 15)], rcv.at[0])
    for step in range(1, 4):
        block = g_ids.at[pl.ds(g * 16, 16)]
        remote(block, block, snd.at[1], rcv.at[1], z * 4 + (g + step) % 4, t)
    for step in range(8):
        to = (t + step) % 8
        src = wo_h.at[:, pl.ds(pl.multiple_of(to * HD, HD), HD)]
        dst = wo.at[pl.ds(pl.multiple_of(t * HD, HD), HD), :]
        if step == 0:
            local(src, dst, rcv.at[5])
        else:
            remote(src, dst, snd.at[5], rcv.at[5], b, to)
    drain(g_ids.at[pl.ds(0, 48)], rcv.at[1])

    for gg in range(4):
        for zh in range(2):
            words = g_ids[pl.ds(gg * 16 + zh * 8, 8), 0, :]
            base = (gg % 2) * 64 + (zh * 2 + gg // 2) * 16
            for r in range(8):
                half = words[:, (r // 4) * 128 : (r // 4) * 128 + 128]
                if r % 4:
                    half = pltpu.roll(half, 128 - 32 * (r % 4), 1)
                for frame in range(2):
                    value = half >> 11 if frame == 0 else half & 2047
                    e_ids[pl.ds(base + frame * 8 + r, 8, stride=128), :] = value.astype(F32)

    def turn(dq, carry):
        start = pl.multiple_of(dq * 128, 128)
        turned = jnp.transpose(e_ids[pl.ds(start, 128), :])
        for book in range(NC):
            idt[book, :, pl.ds(start, 128)] = turned[book : book + 1, :]
        return carry

    lax.fori_loop(0, 8, turn, 0)

    rows_iota = lax.broadcasted_iota(jnp.int32, (VL, VL), 0).astype(F32)

    def one_hot(row):
        return jnp.where(rows_iota == row, 1.0, 0.0).astype(BF16)

    drain(tb, rcv.at[2])
    for k in range(2):
        book = jnp.maximum(2 * mine - 1 + k, 0)
        held = book - jnp.maximum(2 * mine - 1, 0)

        def depth_block(nb, carry, k=k, book=book, held=held):
            start = pl.multiple_of(nb * VL, VL)
            row = idt[book, :, pl.ds(start, VL)]
            total = jnp.zeros((32, VL), F32)
            for part in range(8):
                table = tb[held, :, part * VL : (part + 1) * VL]
                total += jnp.dot(table, one_hot(row - part * VL), preferred_element_type=F32)
            dsum[k * 32 : (k + 1) * 32, pl.ds(start, VL)] = total
            return carry

        lax.fori_loop(0, 4, depth_block, 0)

    def depth_turn(dq, carry):
        block = dsum[:, pl.ds(pl.multiple_of(dq * 128, 128), 128)]
        both = jnp.concatenate([block, pltpu.roll(block, 64, 1)], axis=0)
        tiles = jnp.transpose(both)[0:64, :].astype(BF16)
        sb[pl.ds(dq * 4, 4)] = tiles.reshape(4, 16, 128)
        return carry

    lax.fori_loop(0, 8, depth_turn, 0)

    def place(c):
        return c // 2 % 8 * 4 + c // 16 * 2 + c % 2

    rb_own = local(sb.at[place(chip)], rb.at[chip], rcv.at[6])

    def send_depth(step, carry):
        to = (chip + step) % 32
        remote(sb.at[place(to)], rb.at[chip], snd.at[6], rcv.at[6], to * 2 + core, t)
        return carry

    lax.fori_loop(1, 32, send_depth, 0)

    code_copy.wait()

    def code_block(nb, carry):
        start = pl.multiple_of(nb * VL, VL)

        def add_book(book, total):
            row = idt[book, :, pl.ds(start, VL)] - (t * VL).astype(F32)
            return total + jnp.dot(code_v[book], one_hot(row), preferred_element_type=F32)

        total = lax.fori_loop(0, NC, add_book, jnp.zeros((64, VL), F32), unroll=2)
        cb[pl.ds(nb * 2, 1)] = total[:, 0:128].astype(BF16).reshape(1, 64, 128)
        cb[pl.ds(nb * 2 + 1, 1)] = total[:, 128:256].astype(BF16).reshape(1, 64, 128)
        return carry

    lax.fori_loop(0, 4, code_block, 0)
    local(cb.at[t], cr.at[t], rcv.at[7])
    for step in range(1, 8):
        to = (t + step) % 8
        remote(cb.at[to], cr.at[t], snd.at[7], rcv.at[7], b, to)

    drain(rb, rcv.at[6])
    quarter = lane_iota((16, 128)) // 32

    def gather_features(block, carry):
        tiles = [rb[block * 4 + m].astype(F32) for m in range(4)]
        lanes = pl.ds(pl.multiple_of(block * 128, 128), 128)
        for side in range(2):
            pair = []
            for k in range(2):
                q = side * 2 + k
                out = tiles[q]
                for m in range(4):
                    if m != q:
                        out = jnp.where(quarter == m, pltpu.roll(tiles[m], (m - q) * 32 % 128, 1), out)
                pair.append(out)
            for frame in range(2):
                rows = slice(frame * 8, frame * 8 + 8)
                zb[side, frame, :, lanes] = jnp.concatenate([pair[0][rows], pair[1][rows]], axis=0).astype(BF16)
        return carry

    lax.fori_loop(0, 8, gather_features, 0)
    for frame in range(2):
        for step in range(16):
            to = (mine + step) % 16
            src = zb.at[to % 2, frame]
            dst = xf.at[frame, mine]
            if step == 0:
                local(src, dst, rcv.at[8 + frame])
            else:
                remote(src, dst, snd.at[8 + frame], rcv.at[8 + frame], chip * 2 + to % 2, to // 2)

    drain(cr, rcv.at[7])
    sums = cr[0].astype(F32)
    for part in range(1, 8):
        sums = sums + cr[part].astype(F32)
    high = sums.astype(BF16).astype(F32)
    turned = jnp.transpose(jnp.concatenate([high, sums - high], axis=0))
    cs_src[...] = turned.astype(BF16).reshape(8, 16, 128)
    part_here = b % 8
    owner_t = b // 8
    for side in range(2):
        for d4 in range(4):
            to_b = ((t + 8 * (d4 // 2)) * 2 + d4 % 2) * 2 + side
            src = cs_src.at[side * 4 + d4]
            dst = cs.at[part_here]
            own = jnp.logical_and(to_b == b, owner_t == t)

            @pl.when(own)
            def _(src=src, dst=dst):
                local(src, dst, rcv.at[10])

            @pl.when(jnp.logical_not(own))
            def _(src=src, dst=dst, to_b=to_b):
                remote(src, dst, snd.at[10], rcv.at[10], to_b, owner_t)

    drain(cs, rcv.at[10])
    low_half = lane_iota((8, 128)) < 64
    for frame in range(2):
        for tile in range(4):
            halves = []
            for m in (2 * tile, 2 * tile + 1):
                value = cs[m].astype(F32)[frame * 8 : frame * 8 + 8, :]
                halves.append(value + pltpu.roll(value, 64, 1))
            lanes = slice(tile * 128, tile * 128 + 128)
            stream_v[:, lanes] = stream_v[:, lanes] + jnp.where(low_half, halves[0], halves[1])
        if frame == 0:
            send_leading(1, stream_v[...])
    next_o[...] = stream_v[...]

    dgain_copy.wait()
    drain(wq, loc.at[6])
    head_lanes = pl.ds(pl.multiple_of(t * HD, HD), HD)
    for frame in range(2):
        drain(lb.at[frame, pl.ds(0, 7)], rcv.at[3 + frame])
        total = lb[frame, 0]
        for part in range(1, 8):
            total = total + lb[frame, part]
        scale = lax.rsqrt(total[:, DD : DD + 1] * (1.0 / D) + EPS)
        ld[frame] = total[:, 0:DD] * scale
        drain(xf.at[frame], rcv.at[8 + frame])
        for part in range(4):
            values = xf[frame, part * 4 : part * 4 + 4].reshape(64, DD).astype(F32)
            if part == 0:
                values = jnp.concatenate([ld[frame], values[8:64]], axis=0)
            mean = jnp.sum(values * values, axis=1, keepdims=True) * (1.0 / DD)
            normed = values * lax.rsqrt(mean + EPS) * dgain_v[...]
            nx[part * 64 : part * 64 + 64, :] = normed.astype(BF16)
        qkv = jnp.dot(nx[...], wq[...], preferred_element_type=F32).astype(BF16)
        query, key, value = (qkv[:, p * HD : (p + 1) * HD] for p in range(3))
        scores = lax.dot_general(query, key, (((1,), (1,)), ((), ())), preferred_element_type=F32) * HD ** (-0.5)
        row = lax.broadcasted_iota(jnp.int32, (256, 256), 0)
        col = lax.broadcasted_iota(jnp.int32, (256, 256), 1)
        seen = jnp.logical_and((row & 7) == (col & 7), row >= col)
        scores = jnp.where(seen, scores, -1e30)
        weights = jnp.exp(scores - jnp.max(scores, axis=1, keepdims=True))
        probs = (weights / jnp.sum(weights, axis=1, keepdims=True)).astype(BF16)
        blended = jnp.dot(probs, value, preferred_element_type=F32).astype(BF16)
        bs[frame] = blended
        bl[frame, :, head_lanes] = blended
        for step in range(1, 8):
            remote(bs.at[frame], bl.at[frame, :, head_lanes], snd.at[11 + frame], rcv.at[11 + frame], b, (t + step) % 8)

    drain(wo, rcv.at[5])
    for frame in range(2):
        drain(bl.at[frame, :, pl.ds(0, 7 * HD)], rcv.at[11 + frame])
        out = jnp.dot(bl[frame], wo[...], preferred_element_type=F32)
        held = xf[frame, :, :, head_lanes].reshape(256, HD).astype(F32)
        osum[0:8, :] = out[0:8] + ld[frame, :, head_lanes]
        osum[8:256, :] = out[8:256] + held[8:256]
        for r in range(8):
            states_o[frame, r] = osum[pl.ds(r, 32, stride=8), :].astype(BF16)

    drain(g_ids.at[pl.ds(0, 15)], snd.at[0])
    drain(g_ids.at[pl.ds(0, 48)], snd.at[1])
    drain(xf.at[0, pl.ds(0, 15), :, pl.ds(0, 512)], snd.at[2])
    drain(lb.at[0, pl.ds(0, 7)], snd.at[3])
    drain(lb.at[0, pl.ds(0, 7)], snd.at[4])
    drain(wo.at[pl.ds(0, 7 * HD)], snd.at[5])
    drain(rb.at[pl.ds(0, 31)], snd.at[6])
    drain(cr.at[pl.ds(0, 7)], snd.at[7])
    for frame in range(2):
        drain(xf.at[0, pl.ds(0, 15)], snd.at[8 + frame])
        drain(bl.at[0, :, pl.ds(0, 7 * HD)], snd.at[11 + frame])
    keeps_one = jnp.logical_and(z % 8 == t, owner_t == t)

    @pl.when(keeps_one)
    def _():
        drain(cs.at[pl.ds(0, 7)], snd.at[10])

    @pl.when(jnp.logical_not(keeps_one))
    def _():
        drain(cs, snd.at[10])


def on_device(stream, code_ids, back_gain, projection, code_table, depth_table, depth_gain, qkv_weight, out_weight):
    vm = pltpu.VMEM
    any_space = pl.BlockSpec(memory_space=pl.ANY)
    return pl.pallas_call(
        kernel,
        out_shape=(
            jax.ShapeDtypeStruct((2, 8, NC, HD), BF16),
            jax.ShapeDtypeStruct((8, 512), F32),
        ),
        in_specs=[any_space] * 9,
        out_specs=(pl.BlockSpec(memory_space=vm), pl.BlockSpec(memory_space=vm)),
        scratch_shapes=[
            vm((8, 2, NC), jnp.int32),
            vm((8, 512), F32),
            vm((1, 512), F32),
            vm((512, DD), BF16),
            vm((NC, 64, VL), BF16),
            vm((1, DD), F32),
            vm((DD, 3 * HD), BF16),
            vm((DD, HD), BF16),
            vm((64, 1, 256), jnp.int32),
            vm((1024, 128), F32),
            vm((NC, 1, 1024), F32),
            vm((2, 32, 2048), BF16),
            vm((64, 1024), F32),
            vm((32, 16, 128), BF16),
            vm((32, 16, 128), BF16),
            vm((2, 2, 16, DD), BF16),
            vm((2, 16, 16, DD), BF16),
            vm((256, DD), BF16),
            vm((2, 8, 8, DD + 128), F32),
            vm((2, 8, DD), F32),
            vm((8, 64, 128), BF16),
            vm((8, 64, 128), BF16),
            vm((8, 16, 128), BF16),
            vm((8, 16, 128), BF16),
            vm((2, 256, HD), BF16),
            vm((2, 256, DD), BF16),
            vm((256, HD), F32),
            pltpu.SemaphoreType.DMA((7,)),
            pltpu.SemaphoreType.DMA((13,)),
            pltpu.SemaphoreType.DMA((13,)),
        ],
        compiler_params=pltpu.CompilerParams(
            collective_id=0, has_side_effects=True, vmem_limit_bytes=48 * 1024 * 1024
        ),
    )(
        stream,
        code_ids,
        back_gain.reshape(1, 512),
        projection,
        jnp.swapaxes(code_table, 1, 2),
        jnp.swapaxes(depth_table, 1, 2),
        depth_gain,
        jnp.transpose(qkv_weight[0], (1, 0, 2)),
        out_weight[0],
    )


def solution(mesh):
    return jax.shard_map(
        on_device,
        mesh=mesh,
        in_specs=(
            P("batch", "tensor"),
            P("batch", None, None),
            P("tensor"),
            P("tensor", None),
            P(None, "tensor", "batch"),
            P(None, "tensor", "batch"),
            P(),
            P(None, None, None, "tensor"),
            P(None, "tensor", None),
        ),
        out_specs=(P(None, "batch", None, "tensor"), P("batch", "tensor")),
        check_vma=False,
    )
```

time: 575 us -> 89.8 us (0.16)
  waiting for transfers between devices: 348 us -> 0 us
  blocking collectives: 103 us -> 0 us
  Pallas kernels: 0 us -> 79.2 us
  local copies, waits for them, and re-layouts: 49 us -> 9.51 us
  matrix products: 22.8 us -> 0 us
  starting transfers between devices: 21.9 us -> 0 us
  between operations: 14.4 us -> 0.66 us
  other arithmetic: 11.4 us -> 0 us
    reduce_scatter x5 -> x0, waiting for transfers between devices: 186 us -> none  [the longest x2 97.7 us: on_device(): lax.psum_scatter(partial_out, 'tensor', scatter_dimension=2, tiled=True)]
    all_gather x2 -> x0, waiting for transfers between devices: 94.8 us -> none  [on_device(): full_width = lax.all_gather(residual, 'tensor', axis=2, tiled=True)]
    all_gather x1 -> x0, blocking collectives: 86.4 us -> none  [on_device(): every_code = lax.all_gather(code_ids, 'batch', axis=0, tiled=True)]
    pallas_call x0 -> x1, Pallas kernels: none -> 79.2 us  [on_device(): pl.pallas_call(kernel, out_shape=(jax.ShapeDtypeStruct((2, 8, NC, HD), BF...]
    all_to_all x2 -> x0, waiting for transfers between devices: 50 us -> none  [the longest x1 49.5 us: on_device(): lax.all_to_all(jnp.stack(depth_terms, axis=1), 'batch', split_axis=0, con...]
    unnamed x28 -> x20, local copies, waits for them, and re-layouts: 36.3 us -> 9.51 us
    dot_general x12 -> x0, matrix products: 22.8 us -> none  [the longest x2 6.83 us: on_device(): jnp.einsum('rkv,kvd->rd', one_hot, code_table, preferred_element_type=jnp...]
    all_to_all x2 -> x0, starting transfers between devices: 21.5 us -> none  [the longest x1 14.7 us: on_device(): lax.all_to_all(jnp.stack(depth_terms, axis=1), 'batch', split_axis=0, con...]
  transfers between devices with their start and end apart: 10 -> 0, of which waited for: 9 -> 0; matrix products, arithmetic and copies ran while one was open for 13% -> 0% of each run, Pallas kernels for 0% -> 0%
where the time goes in v1:
time: 89.8 us; the launch traced here: 89.3 us
  Pallas kernels  79.2 us (88%)
  local copies, waits for them, and re-layouts  9.51 us (11%)
    pallas_call x1, Pallas kernels, on_device(): pl.pallas_call(kernel, out_shape=(jax.ShapeDtypeStruct((2, 8, NC, HD), BF...  79.2 us
    unnamed x20, local copies, waits for them, and re-layouts  9.51 us

profile of v1, /device:TPU:1, one launch (start us, length us, event | category | flops | bytes accessed | tf_op | source)
XLA Modules:
  0.0 89.3 jit_solution(6175155362798133000)
XLA Ops:
  0.6 0.0 copy-start.6
  0.6 0.7 copy-done.6
  1.3 0.0 copy-start
  1.3 1.2 %copy-done = bf16[512,1024]{1,0:T(8,128)(2,1)S(1)} copy-done((bf16[512,1024]{1,0:T(8,128)(2,1)S(1)}, bf16[512,1024]{1,0:T(8,128)(2,1)}, u32[]{:S(2)}) %copy-start) | copy-done | bytes 1048600
  2.6 0.0 copy-start.1
  2.6 1.2 %copy-done.1 = bf16[32,256,64]{1,2,0:T(8,128)(2,1)S(1)} copy-done((bf16[32,256,64]{1,2,0:T(8,128)(2,1)S(1)}, bf16[32,256,64]{1,2,0:T(8,128)(2,1)}, u32[]{:S(2)}) %copy-start.1) | copy-done | bytes 1048600
  3.8 0.0 copy-start.2
  3.8 1.1 %copy-done.2 = bf16[1,1024,3,128]{3,1,2,0:T(8,128)(2,1)S(1)} copy-done((bf16[1,1024,3,128]{3,1,2,0:T(8,128)(2,1)S(1)}, bf16[1,1024,3,128]{3,1,2,0:T(8,128)(2,1)}, u32[]{:S(2)}) %copy-start.2) | copy-done | bytes 786456
  4.9 0.0 copy-start.3
  4.9 0.9 %copy-done.3 = bf16[1,128,1024]{2,1,0:T(8,128)(2,1)S(1)} copy-done((bf16[1,128,1024]{2,1,0:T(8,128)(2,1)S(1)}, bf16[1,128,1024]{2,1,0:T(8,128)(2,1)}, u32[]{:S(2)}) %copy-start.3) | copy-done | bytes 262168
  5.9 0.0 copy-start.4
  5.9 0.9 %copy-done.4 = bf16[31,256,16]{1,2,0:T(8,128)(2,1)S(1)} copy-done((bf16[31,256,16]{1,2,0:T(8,128)(2,1)S(1)}, bf16[31,256,16]{1,2,0:T(8,128)(2,1)}, u32[]{:S(2)}) %copy-start.4) | copy-done | bytes 253976
  6.8 0.0 copy-start.5
  6.8 0.7 copy-done.5
  7.5 0.0 copy-start.7
  7.5 0.7 copy-done.7
  8.2 0.0 copy-start.8
  8.2 0.7 copy-done.8
  8.9 79.2 %shard_map.104 = (bf16[2,8,32,128]{3,2,1,0:T(8,128)(2,1)S(1)}, f32[8,512]{1,0:T(8,128)S(1)}) custom-call(f32[8,512]{1,0:T(8,128)S(1)} %copy-done.5, s32[8,2,32]{2,1,0:T(2,128)S(1)} %copy-done.6, f32[1,512]{1,0:T(1,128)S(1)} %bitcast.11, bf16[512,1024]{1,0:T(8,128)(2,1)S(1)} %copy-done, bf16[32,64,256]{2,1,0:T(8,128)(2,1)S(1)} %bitcast.7, ...), custom_call_target="tpu_custom_call" | custom-call | tf_op jit(solution)/shard_map/pallas_call | solution.py:339
  88.1 0.7 copy.13
  88.7 0.6 copy.14
Async XLA Ops:
  0.6 0.7 copy-start.6
  1.3 1.2 %copy-start = (bf16[512,1024]{1,0:T(8,128)(2,1)S(1)}, bf16[512,1024]{1,0:T(8,128)(2,1)}, u32[]{:S(2)}) copy-start(bf16[512,1024]{1,0:T(8,128)(2,1)} %proj_h.1) | copy-start | bytes 3145732
  2.6 1.2 %copy-start.1 = (bf16[32,256,64]{1,2,0:T(8,128)(2,1)S(1)}, bf16[32,256,64]{1,2,0:T(8,128)(2,1)}, u32[]{:S(2)}) copy-start(bf16[32,256,64]{1,2,0:T(8,128)(2,1)} %param.13) | copy-start | bytes 3145732
  3.8 1.1 %copy-start.2 = (bf16[1,1024,3,128]{3,1,2,0:T(8,128)(2,1)S(1)}, bf16[1,1024,3,128]{3,1,2,0:T(8,128)(2,1)}, u32[]{:S(2)}) copy-start(bf16[1,1024,3,128]{3,1,2,0:T(8,128)(2,1)} %param.16) | copy-start | bytes 2359300
  4.9 0.9 %copy-start.3 = (bf16[1,128,1024]{2,1,0:T(8,128)(2,1)S(1)}, bf16[1,128,1024]{2,1,0:T(8,128)(2,1)}, u32[]{:S(2)}) copy-start(bf16[1,128,1024]{2,1,0:T(8,128)(2,1)} %param.17) | copy-start | bytes 786436
  5.9 0.9 %copy-start.4 = (bf16[31,256,16]{1,2,0:T(8,128)(2,1)S(1)}, bf16[31,256,16]{1,2,0:T(8,128)(2,1)}, u32[]{:S(2)}) copy-start(bf16[31,256,16]{1,2,0:T(8,128)(2,1)} %param.14) | copy-start | bytes 761860
  6.8 0.7 copy-start.5
  7.5 0.7 copy-start.7
  8.2 0.7 copy-start.8

commit v2 on v1

v2 whole, which is shorter than its diff:
```python
import jax
import jax.numpy as jnp
from jax import lax
from jax.experimental import pallas as pl
from jax.experimental.pallas import tpu as pltpu
from jax.sharding import PartitionSpec as P

D = 4096
DD = 1024
HD = 128
NC = 32
VL = 256
EPS = 1e-05
MESH = pl.DeviceIdType.MESH
F32 = jnp.float32
BF16 = jnp.bfloat16


def lane_iota(shape):
    return lax.broadcasted_iota(jnp.int32, shape, len(shape) - 1)


def rows_of(t):
    return t % 2 + 2 * ((t // 2 + t // 4) % 2)


def kernel(
    stream_h, ids_h, bgain_h, proj_h, code_h, depth_h, dgain_h, qkv_h, wo_h,
    states_o, next_o,
    ids_v, stream_v, bgain_v, proj_v, code_v, dgain_v, wq, wo,
    g_ids, e_ids, idt, tb, dsum, sb, rb, ms, mb, xm, xa, xs, nx, ls, lr,
    cb, cr, cs_src, cs, po, pt, pr, ob,
    loc, snd, rcv,
):
    b = lax.axis_index("batch")
    t = lax.axis_index("tensor")
    z = b // 4
    g = b % 4
    core = b % 2
    chip = b // 2
    mine = 2 * t + core
    across_core = chip * 2 + 1 - core
    across_xh = z * 4 + (g + 2) % 4
    across_x = t + 1 - 2 * (t % 2)
    across_y = t + 2 - 4 * (t // 2 % 2)
    partner = (3 - t // 2) * 2 + t % 2
    quad = t // 4
    head = t % 4
    pair = rows_of(t)

    def local(src, dst, sem):
        copy = pltpu.make_async_copy(src, dst, sem)
        copy.start()
        return copy

    def remote(src, dst, send_sem, recv_sem, to_b, to_t):
        pltpu.make_async_remote_copy(
            src_ref=src, dst_ref=dst, send_sem=send_sem, recv_sem=recv_sem,
            device_id=(to_b, to_t), device_id_type=MESH,
        ).start()

    def drain(ref, sem):
        pltpu.make_async_copy(ref, ref, sem).wait()

    ids_copy = local(ids_h, ids_v, loc.at[0])

    barrier = pltpu.get_barrier_semaphore()

    def greet(to_b, to_t):
        pl.semaphore_signal(barrier, inc=1, device_id=(to_b, to_t), device_id_type=MESH)

    near = (1, 15, 2, 14, 3, 13, 4, 12)
    for step in near:
        greet((z + step) % 16 * 4 + g, t)
    for step in range(1, 4):
        greet(z * 4 + (g + step) % 4, t)
    for step in range(1, 8):
        for side in range(2):
            greet(chip * 2 + side, (t + step) % 8)
    greet(across_xh, across_x)

    stream_copy = local(stream_h, stream_v, loc.at[1])
    bgain_copy = local(bgain_h, bgain_v, loc.at[2])
    proj_copy = local(proj_h, proj_v, loc.at[3])
    dgain_copy = local(dgain_h, dgain_v, loc.at[5])
    own_lanes = pl.ds(pl.multiple_of(head * HD, HD), HD)
    qkv_copy = local(qkv_h, wq.at[:, :, own_lanes], loc.at[6])
    wo_copy = local(wo_h, wo.at[own_lanes, :], loc.at[7])

    ids_copy.wait()
    slot = g * 16 + z
    packed = ids_v[:, 0, :] * 2048 + ids_v[:, 1, :]
    g_ids[slot] = jnp.concatenate([packed[r : r + 1, :] for r in range(8)], axis=1)

    pl.semaphore_wait(barrier, 26)

    for step in near:
        remote(g_ids.at[slot], g_ids.at[slot], snd.at[0], rcv.at[0], (z + step) % 16 * 4 + g, t)
    for step in range(16):
        to = (mine + step) % 16
        first = jnp.maximum(2 * to - 1, 0)
        src = depth_h.at[pl.ds(first, 2)]
        dst = tb.at[:, pl.ds(pl.multiple_of(core * 16, 16), 16), pl.ds(pl.multiple_of(t * VL, VL), VL)]
        if step == 0:
            local(src, dst, rcv.at[3])
        else:
            remote(src, dst, snd.at[3], rcv.at[3], chip * 2 + to % 2, to // 2)
    own_features = pl.ds(pl.multiple_of(core * 64, 64), 64)
    local(code_h.at[pl.ds(core * 16, 16)], code_v.at[:, own_features, :], loc.at[4])
    remote(code_h.at[pl.ds((1 - core) * 16, 16)], code_v.at[:, own_features, :], snd.at[4], rcv.at[4], across_core, t)

    def quarter_of(part):
        return (
            pl.ds(pl.multiple_of(core * 512 + part * 256, 256), 256),
            pl.ds(pl.multiple_of(core * 64 + part * 32, 32), 32),
        )

    def send_quarter(part, of, from_wq, from_wo, send_sem, recv_sem, to_b, to_t):
        deep, thin = quarter_of(part)
        lanes = pl.ds(pl.multiple_of(of * HD, HD), HD)
        rows = pl.ds(pl.multiple_of(of * HD + core * 64 + part * 32, 32), 32)
        src = qkv_h.at[:, deep, :] if from_wq is None else from_wq.at[:, deep, lanes]
        remote(src, wq.at[:, deep, lanes], send_sem, recv_sem, to_b, to_t)
        src = wo_h.at[thin, :] if from_wo is None else from_wo.at[rows, :]
        remote(src, wo.at[rows, :], send_sem, recv_sem, to_b, to_t)

    for part in range(2):
        send_quarter(part, head, None, None, snd.at[6], rcv.at[6 + part], b, across_y)
    for part in range(2):
        send_quarter(part, head, None, None, snd.at[5], rcv.at[5], (b, across_xh)[part], across_x)

    def forward_across_x(part):
        drain(code_v.at[pl.ds(0, 4)], rcv.at[6 + part])
        send_quarter(part, across_y % 4, wq, wo, snd.at[7], rcv.at[8], (b, across_xh)[part], across_x)

    def share_with_core(of, recv_sem):
        deep = pl.ds(pl.multiple_of(core * 512, 512), 512)
        lanes = pl.ds(pl.multiple_of(of * HD, HD), HD)
        rows = pl.ds(pl.multiple_of(of * HD + core * 64, 64), 64)
        remote(wq.at[:, deep, lanes], wq.at[:, deep, lanes], snd.at[8], recv_sem, across_core, t)
        remote(wo.at[rows, :], wo.at[rows, :], snd.at[8], recv_sem, across_core, t)

    def send_leading(frame, current):
        scaled = (current * bgain_v[...]).astype(BF16)
        partial = jnp.dot(scaled, proj_v[...], preferred_element_type=F32)
        square = jnp.broadcast_to(jnp.sum(current * current, axis=1, keepdims=True), (8, 128))
        for block in range(8):
            ls[frame, pl.ds(block, 8, stride=12), :] = partial[:, block * 128 : block * 128 + 128]
        for block in range(8, 12):
            ls[frame, pl.ds(block, 8, stride=12), :] = square
        for step in range(8):
            to = (t + step) % 8
            src = ls.at[frame, pl.ds(pl.multiple_of(rows_of(to) * 24, 8), 24), :]
            if step == 0:
                local(src, lr.at[frame, t], rcv.at[13 + frame])
            else:
                remote(src, lr.at[frame, t], snd.at[13 + frame], rcv.at[13 + frame], b, to)

    stream_copy.wait()
    bgain_copy.wait()
    proj_copy.wait()
    send_leading(0, stream_v[...])

    drain(g_ids.at[pl.ds(0, 8)], rcv.at[0])
    for side, steps in ((12, (1, 2, 3, 4)), (4, (15, 14, 13))):
        for step in steps:
            item = g_ids.at[g * 16 + (z + step) % 16]
            remote(item, item, snd.at[1], rcv.at[1], (z + side) % 16 * 4 + g, t)
    drain(g_ids.at[pl.ds(0, 7)], rcv.at[1])
    for step in range(1, 4):
        block = g_ids.at[pl.ds(g * 16, 16)]
        remote(block, block, snd.at[2], rcv.at[2], z * 4 + (g + step) % 4, t)
    drain(g_ids.at[pl.ds(0, 48)], rcv.at[2])

    for gg in range(4):
        for zh in range(2):
            words = g_ids[pl.ds(gg * 16 + zh * 8, 8), 0, :]
            base = (gg % 2) * 64 + (zh * 2 + gg // 2) * 16
            for r in range(8):
                half = words[:, (r // 4) * 128 : (r // 4) * 128 + 128]
                if r % 4:
                    half = pltpu.roll(half, 128 - 32 * (r % 4), 1)
                for frame in range(2):
                    value = half >> 11 if frame == 0 else half & 2047
                    e_ids[pl.ds(base + frame * 8 + r, 8, stride=128), :] = value.astype(F32)

    def turn(dq, carry):
        start = pl.multiple_of(dq * 128, 128)
        turned = jnp.transpose(e_ids[pl.ds(start, 128), :])
        for book in range(NC):
            idt[book, :, pl.ds(start, 128)] = turned[book : book + 1, :]
        return carry

    lax.fori_loop(0, 8, turn, 0)

    rows_iota = lax.broadcasted_iota(jnp.int32, (VL, VL), 0).astype(F32)

    def one_hot(row):
        return jnp.where(rows_iota == row, 1.0, 0.0).astype(BF16)

    drain(tb, rcv.at[3])
    for k in range(2):
        book = jnp.maximum(2 * mine - 1 + k, 0)
        held = book - jnp.maximum(2 * mine - 1, 0)

        def depth_block(nb, carry, k=k, book=book, held=held):
            start = pl.multiple_of(nb * VL, VL)
            row = idt[book, :, pl.ds(start, VL)]
            total = jnp.zeros((32, VL), F32)
            for part in range(8):
                table = tb[held, :, part * VL : (part + 1) * VL]
                total += jnp.dot(table, one_hot(row - part * VL), preferred_element_type=F32)
            dsum[k * 32 : (k + 1) * 32, pl.ds(start, VL)] = total
            return carry

        lax.fori_loop(0, 4, depth_block, 0)

    def depth_turn(dq, carry):
        block = dsum[:, pl.ds(pl.multiple_of(dq * 128, 128), 128)]
        both = jnp.concatenate([block, pltpu.roll(block, 64, 1)], axis=0)
        tiles = jnp.transpose(both)[0:64, :].astype(BF16)
        sb[pl.ds(dq * 4, 4)] = tiles.reshape(4, 16, 128)
        return carry

    lax.fori_loop(0, 8, depth_turn, 0)

    def place(c):
        return c // 2 % 8 * 4 + c // 16 * 2 + c % 2

    local(sb.at[place(chip)], rb.at[chip], rcv.at[9])

    def send_depth(step, carry):
        to = (chip + step) % 32
        remote(sb.at[place(to)], rb.at[chip], snd.at[9], rcv.at[9], to * 2 + core, t)
        return carry

    lax.fori_loop(1, 32, send_depth, 0)

    forward_across_x(0)
    drain(code_v.at[pl.ds(0, 8)], rcv.at[5])
    share_with_core(across_x % 4, rcv.at[19])

    drain(code_v.at[pl.ds(0, 8)], loc.at[4])
    drain(code_v.at[pl.ds(0, 8)], rcv.at[4])

    def code_block(nb, carry):
        start = pl.multiple_of(nb * VL, VL)
        total = jnp.zeros((128, VL), F32)
        for book in range(16):
            row = idt[core * 16 + book, :, pl.ds(start, VL)] - (t * VL).astype(F32)
            total += jnp.dot(code_v[book], one_hot(row), preferred_element_type=F32)
        cb[pl.ds(nb * 2, 1)] = total[:, 0:128].astype(BF16).reshape(1, 128, 128)
        cb[pl.ds(nb * 2 + 1, 1)] = total[:, 128:256].astype(BF16).reshape(1, 128, 128)
        return carry

    lax.fori_loop(0, 4, code_block, 0)
    for step in range(16):
        to = (mine + step) % 16
        src = cb.at[to // 2, pl.ds(pl.multiple_of(to % 2 * 64, 64), 64), :]
        if step == 0:
            local(src, cr.at[mine], rcv.at[10])
        else:
            remote(src, cr.at[mine], snd.at[10], rcv.at[10], chip * 2 + to % 2, to // 2)

    forward_across_x(1)
    share_with_core(across_y % 4, rcv.at[20])

    drain(cr, rcv.at[10])
    sums = cr[0].astype(F32)
    for part in range(1, 16):
        sums = sums + cr[part].astype(F32)
    high = sums.astype(BF16).astype(F32)
    turned = jnp.transpose(jnp.concatenate([high, sums - high], axis=0))
    cs_src[...] = turned.astype(BF16).reshape(8, 16, 128)
    owner_t = b // 8
    for side in range(2):
        for d4 in range(4):
            to_b = ((t + 8 * (d4 // 2)) * 2 + d4 % 2) * 2 + side
            src = cs_src.at[side * 4 + d4]
            dst = cs.at[b % 8]
            own = jnp.logical_and(to_b == b, owner_t == t)

            @pl.when(own)
            def _(src=src, dst=dst):
                local(src, dst, rcv.at[12])

            @pl.when(jnp.logical_not(own))
            def _(src=src, dst=dst, to_b=to_b):
                remote(src, dst, snd.at[12], rcv.at[12], to_b, owner_t)

    drain(code_v.at[pl.ds(0, 8)], rcv.at[8])
    share_with_core(3 - head, rcv.at[21])

    drain(rb, rcv.at[9])
    quarter = lane_iota((16, 128)) // 32
    for block in range(8):
        tiles = [rb[block * 4 + m].astype(F32) for m in range(4)]
        for side in range(2):
            for k in range(2):
                q = side * 2 + k
                out = tiles[q]
                for m in range(4):
                    if m != q:
                        out = jnp.where(quarter == m, pltpu.roll(tiles[m], (m - q) * 32 % 128, 1), out)
                for frame in range(2):
                    ms[side, pl.ds(block * 4 + frame * 2 + k, 8, stride=32), :] = out[frame * 8 : frame * 8 + 8]
    mb[...] = ms[...].astype(BF16).reshape(2, 4, 64, 128)
    for step in range(16):
        to = (mine + step) % 16
        src = mb.at[to % 2, rows_of(to // 2)]
        if step == 0:
            local(src, xm.at[mine], rcv.at[11])
        else:
            remote(src, xm.at[mine], snd.at[11], rcv.at[11], chip * 2 + to % 2, to // 2)

    drain(cs, rcv.at[12])
    low_half = lane_iota((8, 128)) < 64
    for frame in range(2):
        for tile in range(4):
            halves = []
            for m in (2 * tile, 2 * tile + 1):
                value = cs[m].astype(F32)[frame * 8 : frame * 8 + 8, :]
                halves.append(value + pltpu.roll(value, 64, 1))
            lanes = slice(tile * 128, tile * 128 + 128)
            stream_v[:, lanes] = stream_v[:, lanes] + jnp.where(low_half, halves[0], halves[1])
        if frame == 0:
            send_leading(1, stream_v[...])
    next_o[...] = stream_v[...]

    drain(xm, rcv.at[11])
    xa[...] = xm[...].astype(F32).reshape(1024, 128)
    for r in range(2):
        for block in range(8):
            for frame in range(2):
                for k in range(2):
                    picked = xa[pl.ds(r * 32 + block * 4 + frame * 2 + k, 16, stride=64), :]
                    xs[block, pl.ds((frame * 2 + r) * 32 + k, 16, stride=2), :] = picked

    dgain_copy.wait()
    qkv_copy.wait()
    wo_copy.wait()
    for shard in range(3):
        drain(code_v.at[pl.ds(0, 8)], rcv.at[19 + shard])

    row = lax.broadcasted_iota(jnp.int32, (64, 64), 0)
    col = lax.broadcasted_iota(jnp.int32, (64, 64), 1)
    seen = jnp.logical_and(row // 32 == col // 32, row >= col)
    own_half = pl.ds(pl.multiple_of(quad * 512, 512), 512)
    other_half = pl.ds(pl.multiple_of((1 - quad) * 512, 512), 512)
    for frame in range(2):
        drain(lr.at[frame], rcv.at[13 + frame])
        total = lr[frame, 0]
        for part in range(1, 8):
            total = total + lr[frame, part]
        for r in range(2):
            scale = lax.rsqrt(total[r * 12 + 8 : r * 12 + 9, :] * (1.0 / D) + EPS)
            for block in range(8):
                line = total[r * 12 + block : r * 12 + block + 1, :] * scale
                at = (frame * 2 + r) * 32
                xs[block, at : at + 1, :] = line
        values = jnp.concatenate([xs[block, frame * 64 : frame * 64 + 64, :] for block in range(8)], axis=1)
        mean = jnp.sum(values * values, axis=1, keepdims=True) * (1.0 / DD)
        nx[...] = (values * lax.rsqrt(mean + EPS) * dgain_v[...]).astype(BF16)
        query, key, value = (
            jnp.dot(nx[...], wq[p], preferred_element_type=F32).astype(BF16) for p in range(3)
        )
        blended = []
        for h in range(4):
            lanes = slice(h * HD, h * HD + HD)
            scores = lax.dot_general(
                query[:, lanes], key[:, lanes], (((1,), (1,)), ((), ())), preferred_element_type=F32
            ) * HD ** (-0.5)
            scores = jnp.where(seen, scores, -1e30)
            weights = jnp.exp(scores - jnp.max(scores, axis=1, keepdims=True))
            probs = (weights / jnp.sum(weights, axis=1, keepdims=True)).astype(BF16)
            blended.append(jnp.dot(probs, value[:, lanes], preferred_element_type=F32).astype(BF16))
        blended = jnp.concatenate(blended, axis=1)
        pt[frame] = jnp.dot(blended, wo[:, other_half], preferred_element_type=F32).astype(BF16)
        remote(pt.at[frame], pr.at[frame], snd.at[15 + frame], rcv.at[15 + frame], b, partner)
        po[frame] = jnp.dot(blended, wo[:, own_half], preferred_element_type=F32)

    for frame in range(2):
        drain(pr.at[frame], rcv.at[15 + frame])
        done = po[frame] + pr[frame].astype(F32)
        for h in range(4):
            kept = xs[quad * 4 + h, frame * 64 : frame * 64 + 64, :]
            ob[frame, h] = (done[:, h * HD : h * HD + HD] + kept).astype(BF16).reshape(2, 32, HD)
        for step in range(4):
            to = (head + step) % 4
            src = ob.at[frame, to]
            dst = states_o.at[frame, pl.ds(pair * 2, 2)]
            if step == 0:
                local(src, dst, rcv.at[17 + frame])
            else:
                remote(src, dst, snd.at[17 + frame], rcv.at[17 + frame], b, quad * 4 + to)
    for frame in range(2):
        drain(states_o.at[frame], rcv.at[17 + frame])

    drain(g_ids.at[pl.ds(0, 8)], snd.at[0])
    drain(g_ids.at[pl.ds(0, 7)], snd.at[1])
    drain(g_ids.at[pl.ds(0, 48)], snd.at[2])
    drain(code_v.at[pl.ds(0, 15), pl.ds(0, 32), :], snd.at[3])
    for which in (4, 5, 6, 7):
        drain(code_v.at[pl.ds(0, 8)], snd.at[which])
    for _ in range(3):
        drain(code_v.at[pl.ds(0, 8)], snd.at[8])
    drain(rb.at[pl.ds(0, 31)], snd.at[9])
    drain(cr.at[pl.ds(0, 15)], snd.at[10])
    drain(xm.at[pl.ds(0, 15)], snd.at[11])
    keeps_one = jnp.logical_and(z % 8 == t, owner_t == t)

    @pl.when(keeps_one)
    def _():
        drain(cs.at[pl.ds(0, 7)], snd.at[12])

    @pl.when(jnp.logical_not(keeps_one))
    def _():
        drain(cs, snd.at[12])

    for frame in range(2):
        drain(lr.at[frame, pl.ds(0, 7)], snd.at[13 + frame])
        drain(pr.at[frame], snd.at[15 + frame])
        drain(ob.at[frame, pl.ds(0, 3)], snd.at[17 + frame])


def on_device(stream, code_ids, back_gain, projection, code_table, depth_table, depth_gain, qkv_weight, out_weight):
    vm = pltpu.VMEM
    in_hbm = pl.BlockSpec(memory_space=pl.ANY)
    return pl.pallas_call(
        kernel,
        out_shape=(
            jax.ShapeDtypeStruct((2, 8, NC, HD), BF16),
            jax.ShapeDtypeStruct((8, 512), F32),
        ),
        in_specs=[in_hbm] * 9,
        out_specs=(pl.BlockSpec(memory_space=vm), pl.BlockSpec(memory_space=vm)),
        scratch_shapes=[
            vm((8, 2, NC), jnp.int32),
            vm((8, 512), F32),
            vm((1, 512), F32),
            vm((512, DD), BF16),
            vm((16, 128, VL), BF16),
            vm((1, DD), F32),
            vm((3, DD, 4 * HD), BF16),
            vm((4 * HD, DD), BF16),
            vm((64, 1, 256), jnp.int32),
            vm((1024, 128), F32),
            vm((NC, 1, 1024), F32),
            vm((2, 32, 2048), BF16),
            vm((64, 1024), F32),
            vm((32, 16, 128), BF16),
            vm((32, 16, 128), BF16),
            vm((2, 256, 128), F32),
            vm((2, 4, 64, 128), BF16),
            vm((16, 64, 128), BF16),
            vm((1024, 128), F32),
            vm((8, 128, 128), F32),
            vm((64, DD), BF16),
            vm((2, 96, 128), F32),
            vm((2, 8, 24, 128), F32),
            vm((8, 128, 128), BF16),
            vm((16, 64, 128), BF16),
            vm((8, 16, 128), BF16),
            vm((8, 16, 128), BF16),
            vm((2, 64, 512), F32),
            vm((2, 64, 512), BF16),
            vm((2, 64, 512), BF16),
            vm((2, 4, 2, 32, HD), BF16),
            pltpu.SemaphoreType.DMA((8,)),
            pltpu.SemaphoreType.DMA((19,)),
            pltpu.SemaphoreType.DMA((22,)),
        ],
        compiler_params=pltpu.CompilerParams(
            collective_id=0, has_side_effects=True, vmem_limit_bytes=60 * 1024 * 1024
        ),
    )(
        stream,
        code_ids,
        back_gain.reshape(1, 512),
        projection,
        jnp.swapaxes(code_table, 1, 2),
        jnp.swapaxes(depth_table, 1, 2),
        depth_gain,
        jnp.transpose(qkv_weight[0], (1, 0, 2)),
        out_weight[0],
    )


def solution(mesh):
    return jax.shard_map(
        on_device,
        mesh=mesh,
        in_specs=(
            P("batch", "tensor"),
            P("batch", None, None),
            P("tensor"),
            P("tensor", None),
            P(None, "tensor", "batch"),
            P(None, "tensor", "batch"),
            P(),
            P(None, None, None, "tensor"),
            P(None, "tensor", None),
        ),
        out_specs=(P(None, "batch", None, "tensor"), P("batch", "tensor")),
        check_vma=False,
    )
```

time: 89.8 us -> 70 us (0.78)
  the two profiles are of different devices: /device:TPU:1 before, /device:TPU:16 now
where the time goes in v2:
time: 70 us; the launch traced here: 69.8 us
  Pallas kernels  67 us (96%)
  local copies, waits for them, and re-layouts  2.18 us (3%)
    pallas_call x1, Pallas kernels, on_device(): pl.pallas_call(kernel, out_shape=(jax.ShapeDtypeStruct((2, 8, NC, HD), BF...  67 us
    unnamed x4, local copies, waits for them, and re-layouts  2.18 us

profile of v2, /device:TPU:16, one launch (start us, length us, event | category | flops | bytes accessed | tf_op | source)
XLA Modules:
  0.0 69.8 jit_solution(14856046096457707056)
XLA Ops:
  0.6 67.0 %shard_map.104 = (bf16[2,8,32,128]{3,2,1,0:T(8,128)(2,1)}, f32[8,512]{1,0:T(8,128)}) custom-call(f32[8,512]{1,0:T(8,128)} %stream_h.1, s32[8,2,32]{2,1,0:T(2,128)} %ids_h.1, f32[1,512]{1,0:T(1,128)} %bitcast.11, bf16[512,1024]{1,0:T(8,128)(2,1)} %proj_h.1, bf16[32,64,256]{2,1,0:T(8,128)(2,1)} %bitcast.7, bf16[31,16,256]{2,1,0:T(8,128)(2,1)} %bitcast.10, ...), custom_call_target="tpu_custom_call" | custom-call | tf_op jit(solution)/shard_map/pallas_call | solution.py:429
  67.7 0.0 copy-start
  67.7 1.6 %copy.13 = bf16[2,8,32,128]{3,2,1,0:T(8,128)(2,1)} copy(bf16[2,8,32,128]{3,2,1,0:T(8,128)(2,1)} %get-tuple-element.4) | data formatting | bytes 262144
  69.2 0.0 copy-done
  69.2 0.6 copy.14
Async XLA Ops:
  67.7 1.6 %copy-start = (f32[8,512]{1,0:T(8,128)S(1)}, f32[8,512]{1,0:T(8,128)}, u32[]{:S(2)}) copy-start(f32[8,512]{1,0:T(8,128)} %get-tuple-element.5) | copy-start | bytes 49156

commit v3 on v2

--- a/solution.py
+++ b/solution.py
@@ -28,7 +28,7 @@
     stream_h, ids_h, bgain_h, proj_h, code_h, depth_h, dgain_h, qkv_h, wo_h,
     states_o, next_o,
     ids_v, stream_v, bgain_v, proj_v, code_v, dgain_v, wq, wo,
-    g_ids, e_ids, idt, tb, dsum, sb, rb, ms, mb, xm, xa, xs, nx, ls, lr,
+    z_ids, g_ids, idt, tb, sb, rb, ms, mb, xm, xa, xs, nx, ls, lr,
     cb, cr, cs_src, cs, po, pt, pr, ob,
     loc, snd, rcv,
 ):
@@ -69,8 +69,7 @@
     def greet(to_b, to_t):
         pl.semaphore_signal(barrier, inc=1, device_id=(to_b, to_t), device_id_type=MESH)
 
-    near = (1, 15, 2, 14, 3, 13, 4, 12)
-    for step in near:
+    for step in range(1, 16):
         greet((z + step) % 16 * 4 + g, t)
     for step in range(1, 4):
         greet(z * 4 + (g + step) % 4, t)
@@ -88,14 +87,13 @@
     wo_copy = local(wo_h, wo.at[own_lanes, :], loc.at[7])
 
     ids_copy.wait()
-    slot = g * 16 + z
-    packed = ids_v[:, 0, :] * 2048 + ids_v[:, 1, :]
-    g_ids[slot] = jnp.concatenate([packed[r : r + 1, :] for r in range(8)], axis=1)
-
-    pl.semaphore_wait(barrier, 26)
-
-    for step in near:
-        remote(g_ids.at[slot], g_ids.at[slot], snd.at[0], rcv.at[0], (z + step) % 16 * 4 + g, t)
+    z_ids[z] = jnp.zeros((8, 128), F32)
+    z_ids[z, :, 0:NC] = (ids_v[:, 0, :] * 2048 + ids_v[:, 1, :]).astype(F32)
+
+    pl.semaphore_wait(barrier, 33)
+
+    for step in range(1, 16):
+        remote(z_ids.at[z], z_ids.at[z], snd.at[0], rcv.at[0], (z + step) % 16 * 4 + g, t)
     for step in range(16):
         to = (mine + step) % 16
         first = jnp.maximum(2 * to - 1, 0)
@@ -106,8 +104,8 @@
         else:
             remote(src, dst, snd.at[3], rcv.at[3], chip * 2 + to % 2, to // 2)
     own_features = pl.ds(pl.multiple_of(core * 64, 64), 64)
-    local(code_h.at[pl.ds(core * 16, 16)], code_v.at[:, own_features, :], loc.at[4])
-    remote(code_h.at[pl.ds((1 - core) * 16, 16)], code_v.at[:, own_features, :], snd.at[4], rcv.at[4], across_core, t)
+    local(code_h, code_v.at[:, own_features, :], loc.at[4])
+    remote(code_h, code_v.at[:, own_features, :], snd.at[4], rcv.at[4], across_core, t)
 
     def quarter_of(part):
         return (
@@ -161,37 +159,21 @@
     proj_copy.wait()
     send_leading(0, stream_v[...])
 
-    drain(g_ids.at[pl.ds(0, 8)], rcv.at[0])
-    for side, steps in ((12, (1, 2, 3, 4)), (4, (15, 14, 13))):
-        for step in steps:
-            item = g_ids.at[g * 16 + (z + step) % 16]
-            remote(item, item, snd.at[1], rcv.at[1], (z + side) % 16 * 4 + g, t)
-    drain(g_ids.at[pl.ds(0, 7)], rcv.at[1])
+    drain(z_ids.at[pl.ds(0, 15)], rcv.at[0])
+    g_ids[g] = jnp.transpose(z_ids[...].reshape(128, 128))[0:NC, :]
     for step in range(1, 4):
-        block = g_ids.at[pl.ds(g * 16, 16)]
-        remote(block, block, snd.at[2], rcv.at[2], z * 4 + (g + step) % 4, t)
-    drain(g_ids.at[pl.ds(0, 48)], rcv.at[2])
-
+        remote(g_ids.at[g], g_ids.at[g], snd.at[2], rcv.at[2], z * 4 + (g + step) % 4, t)
+    drain(g_ids.at[pl.ds(0, 3)], rcv.at[2])
+
+    first_half = lane_iota((NC, 128)) < 64
     for gg in range(4):
-        for zh in range(2):
-            words = g_ids[pl.ds(gg * 16 + zh * 8, 8), 0, :]
-            base = (gg % 2) * 64 + (zh * 2 + gg // 2) * 16
-            for r in range(8):
-                half = words[:, (r // 4) * 128 : (r // 4) * 128 + 128]
-                if r % 4:
-                    half = pltpu.roll(half, 128 - 32 * (r % 4), 1)
-                for frame in range(2):
-                    value = half >> 11 if frame == 0 else half & 2047
-                    e_ids[pl.ds(base + frame * 8 + r, 8, stride=128), :] = value.astype(F32)
-
-    def turn(dq, carry):
-        start = pl.multiple_of(dq * 128, 128)
-        turned = jnp.transpose(e_ids[pl.ds(start, 128), :])
-        for book in range(NC):
-            idt[book, :, pl.ds(start, 128)] = turned[book : book + 1, :]
-        return carry
-
-    lax.fori_loop(0, 8, turn, 0)
+        words = g_ids[gg].astype(jnp.int32)
+        early = (words >> 11).astype(F32)
+        late = (words & 2047).astype(F32)
+        block = gg // 2 * 4 + gg % 2
+        idt[:, block * 128 : block * 128 + 128] = jnp.where(first_half, early, pltpu.roll(late, 64, 1))
+        block = block + 2
+        idt[:, block * 128 : block * 128 + 128] = jnp.where(first_half, pltpu.roll(early, 64, 1), late)
 
     rows_iota = lax.broadcasted_iota(jnp.int32, (VL, VL), 0).astype(F32)
 
@@ -199,97 +181,102 @@
         return jnp.where(rows_iota == row, 1.0, 0.0).astype(BF16)
 
     drain(tb, rcv.at[3])
-    for k in range(2):
-        book = jnp.maximum(2 * mine - 1 + k, 0)
-        held = book - jnp.maximum(2 * mine - 1, 0)
-
-        def depth_block(nb, carry, k=k, book=book, held=held):
-            start = pl.multiple_of(nb * VL, VL)
-            row = idt[book, :, pl.ds(start, VL)]
+    here = g // 2 * 2 + z // 8
+
+    def depth_block(step, carry):
+        nb = (here + step + 1) % 4
+        start = pl.multiple_of(nb * VL, VL)
+        found = []
+        for k in range(2):
+            book = jnp.maximum(2 * mine - 1 + k, 0)
+            held = book - jnp.maximum(2 * mine - 1, 0)
+            row = idt[pl.ds(book, 1), pl.ds(start, VL)]
             total = jnp.zeros((32, VL), F32)
             for part in range(8):
                 table = tb[held, :, part * VL : (part + 1) * VL]
                 total += jnp.dot(table, one_hot(row - part * VL), preferred_element_type=F32)
-            dsum[k * 32 : (k + 1) * 32, pl.ds(start, VL)] = total
-            return carry
-
-        lax.fori_loop(0, 4, depth_block, 0)
-
-    def depth_turn(dq, carry):
-        block = dsum[:, pl.ds(pl.multiple_of(dq * 128, 128), 128)]
-        both = jnp.concatenate([block, pltpu.roll(block, 64, 1)], axis=0)
-        tiles = jnp.transpose(both)[0:64, :].astype(BF16)
-        sb[pl.ds(dq * 4, 4)] = tiles.reshape(4, 16, 128)
+            found.append(total)
+        both = [total[:, side * 128 : side * 128 + 128] for side in range(2) for total in found]
+        turned = jnp.transpose(jnp.concatenate(both, axis=0))
+        for zl in range(8):
+            early, late = turned[zl * 8 : zl * 8 + 8], turned[64 + zl * 8 : 72 + zl * 8]
+            sb[nb * 8 + zl] = jnp.concatenate([early, late], axis=0).astype(BF16)
+        for turn in range(8):
+            zl = (z + turn) % 8
+            to = (nb % 2 * 8 + zl) * 2 + nb // 2
+            src = sb.at[nb * 8 + zl]
+            dst = rb.at[chip]
+            if turn == 0:
+
+                @pl.when(step == 3)
+                def _(src=src, dst=dst):
+                    local(src, dst, rcv.at[9])
+
+                @pl.when(step != 3)
+                def _(src=src, dst=dst, to=to):
+                    remote(src, dst, snd.at[9], rcv.at[9], to * 2 + core, t)
+
+            else:
+                remote(src, dst, snd.at[9], rcv.at[9], to * 2 + core, t)
         return carry
 
-    lax.fori_loop(0, 8, depth_turn, 0)
-
-    def place(c):
-        return c // 2 % 8 * 4 + c // 16 * 2 + c % 2
-
-    local(sb.at[place(chip)], rb.at[chip], rcv.at[9])
-
-    def send_depth(step, carry):
-        to = (chip + step) % 32
-        remote(sb.at[place(to)], rb.at[chip], snd.at[9], rcv.at[9], to * 2 + core, t)
-        return carry
-
-    lax.fori_loop(1, 32, send_depth, 0)
+    lax.fori_loop(0, 4, depth_block, 0)
 
     forward_across_x(0)
     drain(code_v.at[pl.ds(0, 8)], rcv.at[5])
     share_with_core(across_x % 4, rcv.at[19])
 
-    drain(code_v.at[pl.ds(0, 8)], loc.at[4])
-    drain(code_v.at[pl.ds(0, 8)], rcv.at[4])
-
-    def code_block(nb, carry):
-        start = pl.multiple_of(nb * VL, VL)
+    drain(code_v.at[pl.ds(0, 16)], loc.at[4])
+    drain(code_v.at[pl.ds(0, 16)], rcv.at[4])
+
+    def code_block(zh, carry):
+        start = pl.multiple_of((core * 2 + zh) * VL, VL)
         total = jnp.zeros((128, VL), F32)
-        for book in range(16):
-            row = idt[core * 16 + book, :, pl.ds(start, VL)] - (t * VL).astype(F32)
+        for book in range(NC):
+            row = idt[book : book + 1, pl.ds(start, VL)] - (t * VL).astype(F32)
             total += jnp.dot(code_v[book], one_hot(row), preferred_element_type=F32)
-        cb[pl.ds(nb * 2, 1)] = total[:, 0:128].astype(BF16).reshape(1, 128, 128)
-        cb[pl.ds(nb * 2 + 1, 1)] = total[:, 128:256].astype(BF16).reshape(1, 128, 128)
+        total = total.astype(BF16)
+        for side in range(2):
+            for i in range(2):
+                cb[side * 4 + zh * 2 + i] = total[i * 64 : i * 64 + 64, side * 128 : side * 128 + 128]
         return carry
 
-    lax.fori_loop(0, 4, code_block, 0)
-    for step in range(16):
-        to = (mine + step) % 16
-        src = cb.at[to // 2, pl.ds(pl.multiple_of(to % 2 * 64, 64), 64), :]
+    lax.fori_loop(0, 2, code_block, 0)
+    for step in range(8):
+        to = (t + step) % 8
         if step == 0:
-            local(src, cr.at[mine], rcv.at[10])
+            local(cb.at[to], cr.at[t], rcv.at[10])
         else:
-            remote(src, cr.at[mine], snd.at[10], rcv.at[10], chip * 2 + to % 2, to // 2)
-
-    forward_across_x(1)
-    share_with_core(across_y % 4, rcv.at[20])
+            remote(cb.at[to], cr.at[t], snd.at[10], rcv.at[10], b, to)
 
     drain(cr, rcv.at[10])
     sums = cr[0].astype(F32)
-    for part in range(1, 16):
+    for part in range(1, 8):
         sums = sums + cr[part].astype(F32)
     high = sums.astype(BF16).astype(F32)
     turned = jnp.transpose(jnp.concatenate([high, sums - high], axis=0))
-    cs_src[...] = turned.astype(BF16).reshape(8, 16, 128)
-    owner_t = b // 8
-    for side in range(2):
-        for d4 in range(4):
-            to_b = ((t + 8 * (d4 // 2)) * 2 + d4 % 2) * 2 + side
-            src = cs_src.at[side * 4 + d4]
-            dst = cs.at[b % 8]
-            own = jnp.logical_and(to_b == b, owner_t == t)
-
-            @pl.when(own)
-            def _(src=src, dst=dst):
-                local(src, dst, rcv.at[12])
-
-            @pl.when(jnp.logical_not(own))
-            def _(src=src, dst=dst, to_b=to_b):
-                remote(src, dst, snd.at[12], rcv.at[12], to_b, owner_t)
-
-    drain(code_v.at[pl.ds(0, 8)], rcv.at[8])
-    share_with_core(3 - head, rcv.at[21])
+    for zl in range(8):
+        early, late = turned[zl * 8 : zl * 8 + 8], turned[64 + zl * 8 : 72 + zl * 8]
+        cs_src[zl] = jnp.concatenate([early, late], axis=0).astype(BF16)
+    owner_t = chip // 4
+    to_g = core * 2 + t // 4
+    for turn in range(8):
+        zl = (z + turn) % 8
+        to_b = (t // 2 % 2 * 8 + zl) * 4 + to_g
+        src = cs_src.at[zl]
+        dst = cs.at[(chip * 2 + t % 2) % 8]
+        own = jnp.logical_and(to_b == b, owner_t == t)
+
+        @pl.when(own)
+        def _(src=src, dst=dst):
+            local(src, dst, rcv.at[12])
+
+        @pl.when(jnp.logical_not(own))
+        def _(src=src, dst=dst, to_b=to_b):
+            remote(src, dst, snd.at[12], rcv.at[12], to_b, owner_t)
+
+    forward_across_x(1)
+    share_with_core(across_y % 4, rcv.at[20])
 
     drain(rb, rcv.at[9])
     quarter = lane_iota((16, 128)) // 32
@@ -312,6 +299,9 @@
             local(src, xm.at[mine], rcv.at[11])
         else:
             remote(src, xm.at[mine], snd.at[11], rcv.at[11], chip * 2 + to % 2, to // 2)
+
+    drain(code_v.at[pl.ds(0, 8)], rcv.at[8])
+    share_with_core(3 - head, rcv.at[21])
 
     drain(cs, rcv.at[12])
     low_half = lane_iota((8, 128)) < 64
@@ -396,18 +386,18 @@
     for frame in range(2):
         drain(states_o.at[frame], rcv.at[17 + frame])
 
-    drain(g_ids.at[pl.ds(0, 8)], snd.at[0])
-    drain(g_ids.at[pl.ds(0, 7)], snd.at[1])
-    drain(g_ids.at[pl.ds(0, 48)], snd.at[2])
+    drain(z_ids.at[pl.ds(0, 15)], snd.at[0])
+    drain(g_ids.at[pl.ds(0, 3)], snd.at[2])
     drain(code_v.at[pl.ds(0, 15), pl.ds(0, 32), :], snd.at[3])
-    for which in (4, 5, 6, 7):
+    drain(code_v.at[pl.ds(0, 16)], snd.at[4])
+    for which in (5, 6, 7):
         drain(code_v.at[pl.ds(0, 8)], snd.at[which])
     for _ in range(3):
         drain(code_v.at[pl.ds(0, 8)], snd.at[8])
     drain(rb.at[pl.ds(0, 31)], snd.at[9])
-    drain(cr.at[pl.ds(0, 15)], snd.at[10])
+    drain(cr.at[pl.ds(0, 7)], snd.at[10])
     drain(xm.at[pl.ds(0, 15)], snd.at[11])
-    keeps_one = jnp.logical_and(z % 8 == t, owner_t == t)
+    keeps_one = jnp.logical_and(jnp.logical_and(t // 2 % 2 == z // 8, to_g == g), owner_t == t)
 
     @pl.when(keeps_one)
     def _():
@@ -439,15 +429,14 @@
             vm((8, 512), F32),
             vm((1, 512), F32),
             vm((512, DD), BF16),
-            vm((16, 128, VL), BF16),
+            vm((NC, 128, VL), BF16),
             vm((1, DD), F32),
             vm((3, DD, 4 * HD), BF16),
             vm((4 * HD, DD), BF16),
-            vm((64, 1, 256), jnp.int32),
-            vm((1024, 128), F32),
-            vm((NC, 1, 1024), F32),
+            vm((16, 8, 128), F32),
+            vm((4, NC, 128), F32),
+            vm((NC, 1024), F32),
             vm((2, 32, 2048), BF16),
-            vm((64, 1024), F32),
             vm((32, 16, 128), BF16),
             vm((32, 16, 128), BF16),
             vm((2, 256, 128), F32),
@@ -458,8 +447,8 @@
             vm((64, DD), BF16),
             vm((2, 96, 128), F32),
             vm((2, 8, 24, 128), F32),
-            vm((8, 128, 128), BF16),
-            vm((16, 64, 128), BF16),
+            vm((8, 64, 128), BF16),
+            vm((8, 64, 128), BF16),
             vm((8, 16, 128), BF16),
             vm((8, 16, 128), BF16),
             vm((2, 64, 512), F32),

time: 70 us -> 68.5 us (0.979)
  Pallas kernels: 67 us -> 65.5 us
    pallas_call x1, Pallas kernels: 67 us -> 65.5 us  [on_device(): pl.pallas_call(kernel, out_shape=(jax.ShapeDtypeStruct((2, 8, NC, HD), BF...]
where the time goes in v3:
time: 68.5 us; the launch traced here: 68.3 us
  Pallas kernels  65.5 us (96%)
  local copies, waits for them, and re-layouts  2.18 us (3%)
    pallas_call x1, Pallas kernels, on_device(): pl.pallas_call(kernel, out_shape=(jax.ShapeDtypeStruct((2, 8, NC, HD), BF...  65.5 us
    unnamed x4, local copies, waits for them, and re-layouts  2.18 us

profile of v3, /device:TPU:16, one launch (start us, length us, event | category | flops | bytes accessed | tf_op | source)
XLA Modules:
  0.0 68.3 jit_solution(8571239673110443174)
XLA Ops:
  0.6 65.5 %shard_map.104 = (bf16[2,8,32,128]{3,2,1,0:T(8,128)(2,1)}, f32[8,512]{1,0:T(8,128)}) custom-call(f32[8,512]{1,0:T(8,128)} %stream_h.1, s32[8,2,32]{2,1,0:T(2,128)} %ids_h.1, f32[1,512]{1,0:T(1,128)} %bitcast.11, bf16[512,1024]{1,0:T(8,128)(2,1)} %proj_h.1, bf16[32,64,256]{2,1,0:T(8,128)(2,1)} %bitcast.7, bf16[31,16,256]{2,1,0:T(8,128)(2,1)} %bitcast.10, ...), custom_call_target="tpu_custom_call" | custom-call | tf_op jit(solution)/shard_map/pallas_call | solution.py:419
  66.1 0.0 copy-start
  66.1 1.6 %copy.13 = bf16[2,8,32,128]{3,2,1,0:T(8,128)(2,1)} copy(bf16[2,8,32,128]{3,2,1,0:T(8,128)(2,1)} %get-tuple-element.4) | data formatting | bytes 262144
  67.7 0.0 copy-done
  67.7 0.6 copy.14
Async XLA Ops:
  66.1 1.6 %copy-start = (f32[8,512]{1,0:T(8,128)S(1)}, f32[8,512]{1,0:T(8,128)}, u32[]{:S(2)}) copy-start(f32[8,512]{1,0:T(8,128)} %get-tuple-element.5) | copy-start | bytes 49156

commit v4 on v3

--- a/solution.py
+++ b/solution.py
@@ -28,8 +28,8 @@
     stream_h, ids_h, bgain_h, proj_h, code_h, depth_h, dgain_h, qkv_h, wo_h,
     states_o, next_o,
     ids_v, stream_v, bgain_v, proj_v, code_v, dgain_v, wq, wo,
-    z_ids, g_ids, idt, tb, sb, rb, ms, mb, xm, xa, xs, nx, ls, lr,
-    cb, cr, cs_src, cs, po, pt, pr, ob,
+    ids_all, e_ids, idt, tb, sb, rb, ms, mb, xm, xa, xs, nx, ls, lr,
+    cb, cr, cs_src, cs, ob, fr, so,
     loc, snd, rcv,
 ):
     b = lax.axis_index("batch")
@@ -43,7 +43,6 @@
     across_xh = z * 4 + (g + 2) % 4
     across_x = t + 1 - 2 * (t % 2)
     across_y = t + 2 - 4 * (t // 2 % 2)
-    partner = (3 - t // 2) * 2 + t % 2
     quad = t // 4
     head = t % 4
     pair = rows_of(t)
@@ -69,10 +68,11 @@
     def greet(to_b, to_t):
         pl.semaphore_signal(barrier, inc=1, device_id=(to_b, to_t), device_id_type=MESH)
 
-    for step in range(1, 16):
-        greet((z + step) % 16 * 4 + g, t)
-    for step in range(1, 4):
-        greet(z * 4 + (g + step) % 4, t)
+    def greet_batch(step, carry):
+        greet((b + step) % 64, t)
+        return carry
+
+    lax.fori_loop(1, 64, greet_batch, 0)
     for step in range(1, 8):
         for side in range(2):
             greet(chip * 2 + side, (t + step) % 8)
@@ -87,13 +87,17 @@
     wo_copy = local(wo_h, wo.at[own_lanes, :], loc.at[7])
 
     ids_copy.wait()
-    z_ids[z] = jnp.zeros((8, 128), F32)
-    z_ids[z, :, 0:NC] = (ids_v[:, 0, :] * 2048 + ids_v[:, 1, :]).astype(F32)
-
-    pl.semaphore_wait(barrier, 33)
-
-    for step in range(1, 16):
-        remote(z_ids.at[z], z_ids.at[z], snd.at[0], rcv.at[0], (z + step) % 16 * 4 + g, t)
+    slot = g * 16 + z
+    packed = ids_v[:, 0, :] * 2048 + ids_v[:, 1, :]
+    ids_all[slot] = jnp.concatenate([packed[r : r + 1, :] for r in range(8)], axis=1)
+
+    pl.semaphore_wait(barrier, 78)
+
+    def send_ids(step, carry):
+        remote(ids_all.at[slot], ids_all.at[slot], snd.at[0], rcv.at[0], (b + step) % 64, t)
+        return carry
+
+    lax.fori_loop(1, 64, send_ids, 0)
     for step in range(16):
         to = (mine + step) % 16
         first = jnp.maximum(2 * to - 1, 0)
@@ -124,9 +128,6 @@
 
     for part in range(2):
         send_quarter(part, head, None, None, snd.at[6], rcv.at[6 + part], b, across_y)
-    for part in range(2):
-        send_quarter(part, head, None, None, snd.at[5], rcv.at[5], (b, across_xh)[part], across_x)
-
     def forward_across_x(part):
         drain(code_v.at[pl.ds(0, 4)], rcv.at[6 + part])
         send_quarter(part, across_y % 4, wq, wo, snd.at[7], rcv.at[8], (b, across_xh)[part], across_x)
@@ -159,15 +160,21 @@
     proj_copy.wait()
     send_leading(0, stream_v[...])
 
-    drain(z_ids.at[pl.ds(0, 15)], rcv.at[0])
-    g_ids[g] = jnp.transpose(z_ids[...].reshape(128, 128))[0:NC, :]
-    for step in range(1, 4):
-        remote(g_ids.at[g], g_ids.at[g], snd.at[2], rcv.at[2], z * 4 + (g + step) % 4, t)
-    drain(g_ids.at[pl.ds(0, 3)], rcv.at[2])
-
+    drain(ids_all.at[pl.ds(0, 63)], rcv.at[0])
+    for part in range(2):
+        send_quarter(part, head, None, None, snd.at[5], rcv.at[5], (b, across_xh)[part], across_x)
+
+    for gg in range(4):
+        for zh in range(2):
+            words = ids_all[pl.ds(gg * 16 + zh * 8, 8), 0, :]
+            for r in range(8):
+                half = words[:, r // 4 * 128 : r // 4 * 128 + 128]
+                if r % 4:
+                    half = pltpu.roll(half, 128 - 32 * (r % 4), 1)
+                e_ids[gg, pl.ds(zh * 64 + r, 8, stride=8), :] = half.astype(F32)
     first_half = lane_iota((NC, 128)) < 64
     for gg in range(4):
-        words = g_ids[gg].astype(jnp.int32)
+        words = jnp.transpose(e_ids[gg])[0:NC, :].astype(jnp.int32)
         early = (words >> 11).astype(F32)
         late = (words & 2047).astype(F32)
         block = gg // 2 * 4 + gg % 2
@@ -315,7 +322,7 @@
             stream_v[:, lanes] = stream_v[:, lanes] + jnp.where(low_half, halves[0], halves[1])
         if frame == 0:
             send_leading(1, stream_v[...])
-    next_o[...] = stream_v[...]
+    local(stream_v, next_o, loc.at[1])
 
     drain(xm, rcv.at[11])
     xa[...] = xm[...].astype(F32).reshape(1024, 128)
@@ -335,8 +342,6 @@
     row = lax.broadcasted_iota(jnp.int32, (64, 64), 0)
     col = lax.broadcasted_iota(jnp.int32, (64, 64), 1)
     seen = jnp.logical_and(row // 32 == col // 32, row >= col)
-    own_half = pl.ds(pl.multiple_of(quad * 512, 512), 512)
-    other_half = pl.ds(pl.multiple_of((1 - quad) * 512, 512), 512)
     for frame in range(2):
         drain(lr.at[frame], rcv.at[13 + frame])
         total = lr[frame, 0]
@@ -365,29 +370,29 @@
             probs = (weights / jnp.sum(weights, axis=1, keepdims=True)).astype(BF16)
             blended.append(jnp.dot(probs, value[:, lanes], preferred_element_type=F32).astype(BF16))
         blended = jnp.concatenate(blended, axis=1)
-        pt[frame] = jnp.dot(blended, wo[:, other_half], preferred_element_type=F32).astype(BF16)
-        remote(pt.at[frame], pr.at[frame], snd.at[15 + frame], rcv.at[15 + frame], b, partner)
-        po[frame] = jnp.dot(blended, wo[:, own_half], preferred_element_type=F32)
+        added = jnp.dot(blended, wo[...], preferred_element_type=F32)
+        for to in range(8):
+            part = added[:, to * HD : to * HD + HD]
+            part = jnp.where(quad == to // 4, part + xs[to, frame * 64 : frame * 64 + 64, :], part)
+            ob[frame, to] = part.astype(BF16).reshape(2, 32, HD)
+        for step in range(8):
+            to = (t + step) % 8
+            src = ob.at[frame, to]
+            dst = fr.at[frame, quad, pl.ds(pair * 2, 2)]
+            if step == 0:
+                local(src, dst, rcv.at[15 + frame])
+            else:
+                remote(src, dst, snd.at[15 + frame], rcv.at[15 + frame], b, to)
 
     for frame in range(2):
-        drain(pr.at[frame], rcv.at[15 + frame])
-        done = po[frame] + pr[frame].astype(F32)
-        for h in range(4):
-            kept = xs[quad * 4 + h, frame * 64 : frame * 64 + 64, :]
-            ob[frame, h] = (done[:, h * HD : h * HD + HD] + kept).astype(BF16).reshape(2, 32, HD)
-        for step in range(4):
-            to = (head + step) % 4
-            src = ob.at[frame, to]
-            dst = states_o.at[frame, pl.ds(pair * 2, 2)]
-            if step == 0:
-                local(src, dst, rcv.at[17 + frame])
-            else:
-                remote(src, dst, snd.at[17 + frame], rcv.at[17 + frame], b, quad * 4 + to)
+        drain(fr.at[frame], rcv.at[15 + frame])
+        so[frame] = (fr[frame, 0].astype(F32) + fr[frame, 1].astype(F32)).astype(BF16)
+        local(so.at[frame], states_o.at[frame], loc.at[2 + frame])
+
+    drain(stream_v, loc.at[1])
     for frame in range(2):
-        drain(states_o.at[frame], rcv.at[17 + frame])
-
-    drain(z_ids.at[pl.ds(0, 15)], snd.at[0])
-    drain(g_ids.at[pl.ds(0, 3)], snd.at[2])
+        drain(so.at[frame], loc.at[2 + frame])
+    drain(ids_all.at[pl.ds(0, 63)], snd.at[0])
     drain(code_v.at[pl.ds(0, 15), pl.ds(0, 32), :], snd.at[3])
     drain(code_v.at[pl.ds(0, 16)], snd.at[4])
     for which in (5, 6, 7):
@@ -409,8 +414,7 @@
 
     for frame in range(2):
         drain(lr.at[frame, pl.ds(0, 7)], snd.at[13 + frame])
-        drain(pr.at[frame], snd.at[15 + frame])
-        drain(ob.at[frame, pl.ds(0, 3)], snd.at[17 + frame])
+        drain(ob.at[frame, pl.ds(0, 7)], snd.at[15 + frame])
 
 
 def on_device(stream, code_ids, back_gain, projection, code_table, depth_table, depth_gain, qkv_weight, out_weight):
@@ -423,7 +427,7 @@
             jax.ShapeDtypeStruct((8, 512), F32),
         ),
         in_specs=[in_hbm] * 9,
-        out_specs=(pl.BlockSpec(memory_space=vm), pl.BlockSpec(memory_space=vm)),
+        out_specs=(in_hbm, in_hbm),
         scratch_shapes=[
             vm((8, 2, NC), jnp.int32),
             vm((8, 512), F32),
@@ -433,8 +437,8 @@
             vm((1, DD), F32),
             vm((3, DD, 4 * HD), BF16),
             vm((4 * HD, DD), BF16),
-            vm((16, 8, 128), F32),
-            vm((4, NC, 128), F32),
+            vm((64, 1, 256), jnp.int32),
+            vm((4, 128, 128), F32),
             vm((NC, 1024), F32),
             vm((2, 32, 2048), BF16),
             vm((32, 16, 128), BF16),
@@ -451,10 +455,9 @@
             vm((8, 64, 128), BF16),
             vm((8, 16, 128), BF16),
             vm((8, 16, 128), BF16),
-            vm((2, 64, 512), F32),
-            vm((2, 64, 512), BF16),
-            vm((2, 64, 512), BF16),
-            vm((2, 4, 2, 32, HD), BF16),
+            vm((2, 8, 2, 32, HD), BF16),
+            vm((2, 2, 8, 32, HD), BF16),
+            vm((2, 8, 32, HD), BF16),
             pltpu.SemaphoreType.DMA((8,)),
             pltpu.SemaphoreType.DMA((19,)),
             pltpu.SemaphoreType.DMA((22,)),

time: 68.5 us -> 69.6 us (1.016)
  the two profiles are of different devices: /device:TPU:16 before, /device:TPU:24 now
where the time goes in v4:
time: 69.6 us; the launch traced here: 69.4 us
  Pallas kernels  66.6 us (96%)
  local copies, waits for them, and re-layouts  2.18 us (3%)
    pallas_call x1, Pallas kernels, on_device(): pl.pallas_call(kernel, out_shape=(jax.ShapeDtypeStruct((2, 8, NC, HD), BF...  66.6 us
    unnamed x4, local copies, waits for them, and re-layouts  2.18 us

profile of v4, /device:TPU:24, one launch (start us, length us, event | category | flops | bytes accessed | tf_op | source)
XLA Modules:
  0.0 69.4 jit_solution(6983834323348590799)
XLA Ops:
  0.6 66.6 %shard_map.104 = (bf16[2,8,32,128]{3,2,1,0:T(8,128)(2,1)}, f32[8,512]{1,0:T(8,128)}) custom-call(f32[8,512]{1,0:T(8,128)} %stream_h.1, s32[8,2,32]{2,1,0:T(2,128)} %ids_h.1, f32[1,512]{1,0:T(1,128)} %bitcast.11, bf16[512,1024]{1,0:T(8,128)(2,1)} %proj_h.1, bf16[32,64,256]{2,1,0:T(8,128)(2,1)} %bitcast.7, bf16[31,16,256]{2,1,0:T(8,128)(2,1)} %bitcast.10, ...), custom_call_target="tpu_custom_call" | custom-call | tf_op jit(solution)/shard_map/pallas_call | solution.py:423
  67.2 0.0 copy-start
  67.3 1.6 %copy.13 = bf16[2,8,32,128]{3,2,1,0:T(8,128)(2,1)} copy(bf16[2,8,32,128]{3,2,1,0:T(8,128)(2,1)} %get-tuple-element.4) | data formatting | bytes 262144
  68.8 0.0 copy-done
  68.8 0.6 copy.14
Async XLA Ops:
  67.2 1.6 %copy-start = (f32[8,512]{1,0:T(8,128)S(1)}, f32[8,512]{1,0:T(8,128)}, u32[]{:S(2)}) copy-start(f32[8,512]{1,0:T(8,128)} %get-tuple-element.5) | copy-start | bytes 49156

commit v5 on v4

--- a/solution.py
+++ b/solution.py
@@ -21,7 +21,7 @@
 
 
 def rows_of(t):
-    return t % 2 + 2 * ((t // 2 + t // 4) % 2)
+    return t // 2
 
 
 def kernel(
@@ -40,11 +40,10 @@
     chip = b // 2
     mine = 2 * t + core
     across_core = chip * 2 + 1 - core
-    across_xh = z * 4 + (g + 2) % 4
-    across_x = t + 1 - 2 * (t % 2)
-    across_y = t + 2 - 4 * (t // 2 % 2)
-    quad = t // 4
-    head = t % 4
+    up = (t + 2) % 8
+    down = (t + 6) % 8
+    quad = t % 2
+    head = t // 2
     pair = rows_of(t)
 
     def local(src, dst, sem):
@@ -76,7 +75,6 @@
     for step in range(1, 8):
         for side in range(2):
             greet(chip * 2 + side, (t + step) % 8)
-    greet(across_xh, across_x)
 
     stream_copy = local(stream_h, stream_v, loc.at[1])
     bgain_copy = local(bgain_h, bgain_v, loc.at[2])
@@ -91,7 +89,7 @@
     packed = ids_v[:, 0, :] * 2048 + ids_v[:, 1, :]
     ids_all[slot] = jnp.concatenate([packed[r : r + 1, :] for r in range(8)], axis=1)
 
-    pl.semaphore_wait(barrier, 78)
+    pl.semaphore_wait(barrier, 77)
 
     def send_ids(step, carry):
         remote(ids_all.at[slot], ids_all.at[slot], snd.at[0], rcv.at[0], (b + step) % 64, t)
@@ -127,10 +125,8 @@
         remote(src, wo.at[rows, :], send_sem, recv_sem, to_b, to_t)
 
     for part in range(2):
-        send_quarter(part, head, None, None, snd.at[6], rcv.at[6 + part], b, across_y)
-    def forward_across_x(part):
-        drain(code_v.at[pl.ds(0, 4)], rcv.at[6 + part])
-        send_quarter(part, across_y % 4, wq, wo, snd.at[7], rcv.at[8], (b, across_xh)[part], across_x)
+        send_quarter(part, head, None, None, snd.at[5], rcv.at[5 + part], b, up)
+        send_quarter(1 - part, head, None, None, snd.at[6], rcv.at[8 - part], b, down)
 
     def share_with_core(of, recv_sem):
         deep = pl.ds(pl.multiple_of(core * 512, 512), 512)
@@ -161,8 +157,6 @@
     send_leading(0, stream_v[...])
 
     drain(ids_all.at[pl.ds(0, 63)], rcv.at[0])
-    for part in range(2):
-        send_quarter(part, head, None, None, snd.at[5], rcv.at[5], (b, across_xh)[part], across_x)
 
     for gg in range(4):
         for zh in range(2):
@@ -186,6 +180,29 @@
 
     def one_hot(row):
         return jnp.where(rows_iota == row, 1.0, 0.0).astype(BF16)
+
+    drain(code_v.at[pl.ds(0, 16)], loc.at[4])
+    drain(code_v.at[pl.ds(0, 16)], rcv.at[4])
+
+    def code_block(zh, carry):
+        start = pl.multiple_of((core * 2 + zh) * VL, VL)
+        total = jnp.zeros((128, VL), F32)
+        for book in range(NC):
+            row = idt[book : book + 1, pl.ds(start, VL)] - (t * VL).astype(F32)
+            total += jnp.dot(code_v[book], one_hot(row), preferred_element_type=F32)
+        total = total.astype(BF16)
+        for side in range(2):
+            for i in range(2):
+                cb[side * 4 + zh * 2 + i] = total[i * 64 : i * 64 + 64, side * 128 : side * 128 + 128]
+        return carry
+
+    lax.fori_loop(0, 2, code_block, 0)
+    for step in range(8):
+        to = (t + step) % 8
+        if step == 0:
+            local(cb.at[to], cr.at[t], rcv.at[10])
+        else:
+            remote(cb.at[to], cr.at[t], snd.at[10], rcv.at[10], b, to)
 
     drain(tb, rcv.at[3])
     here = g // 2 * 2 + z // 8
@@ -229,32 +246,6 @@
 
     lax.fori_loop(0, 4, depth_block, 0)
 
-    forward_across_x(0)
-    drain(code_v.at[pl.ds(0, 8)], rcv.at[5])
-    share_with_core(across_x % 4, rcv.at[19])
-
-    drain(code_v.at[pl.ds(0, 16)], loc.at[4])
-    drain(code_v.at[pl.ds(0, 16)], rcv.at[4])
-
-    def code_block(zh, carry):
-        start = pl.multiple_of((core * 2 + zh) * VL, VL)
-        total = jnp.zeros((128, VL), F32)
-        for book in range(NC):
-            row = idt[book : book + 1, pl.ds(start, VL)] - (t * VL).astype(F32)
-            total += jnp.dot(code_v[book], one_hot(row), preferred_element_type=F32)
-        total = total.astype(BF16)
-        for side in range(2):
-            for i in range(2):
-                cb[side * 4 + zh * 2 + i] = total[i * 64 : i * 64 + 64, side * 128 : side * 128 + 128]
-        return carry
-
-    lax.fori_loop(0, 2, code_block, 0)
-    for step in range(8):
-        to = (t + step) % 8
-        if step == 0:
-            local(cb.at[to], cr.at[t], rcv.at[10])
-        else:
-            remote(cb.at[to], cr.at[t], snd.at[10], rcv.at[10], b, to)
 
     drain(cr, rcv.at[10])
     sums = cr[0].astype(F32)
@@ -282,8 +273,14 @@
         def _(src=src, dst=dst, to_b=to_b):
             remote(src, dst, snd.at[12], rcv.at[12], to_b, owner_t)
 
-    forward_across_x(1)
-    share_with_core(across_y % 4, rcv.at[20])
+    drain(code_v.at[pl.ds(0, 4)], rcv.at[5])
+    send_quarter(0, down // 2, wq, wo, snd.at[7], rcv.at[17], b, up)
+    drain(code_v.at[pl.ds(0, 4)], rcv.at[8])
+    send_quarter(1, up // 2, wq, wo, snd.at[7], rcv.at[17], b, down)
+    drain(code_v.at[pl.ds(0, 4)], rcv.at[6])
+    share_with_core(down // 2, rcv.at[19])
+    drain(code_v.at[pl.ds(0, 4)], rcv.at[7])
+    share_with_core(up // 2, rcv.at[20])
 
     drain(rb, rcv.at[9])
     quarter = lane_iota((16, 128)) // 32
@@ -307,8 +304,6 @@
         else:
             remote(src, xm.at[mine], snd.at[11], rcv.at[11], chip * 2 + to % 2, to // 2)
 
-    drain(code_v.at[pl.ds(0, 8)], rcv.at[8])
-    share_with_core(3 - head, rcv.at[21])
 
     drain(cs, rcv.at[12])
     low_half = lane_iota((8, 128)) < 64
@@ -323,6 +318,9 @@
         if frame == 0:
             send_leading(1, stream_v[...])
     local(stream_v, next_o, loc.at[1])
+
+    drain(code_v.at[pl.ds(0, 8)], rcv.at[17])
+    share_with_core((head + 2) % 4, rcv.at[21])
 
     drain(xm, rcv.at[11])
     xa[...] = xm[...].astype(F32).reshape(1024, 128)

time: 69.6 us -> 65.2 us (0.937)
  the two profiles are of different devices: /device:TPU:24 before, /device:TPU:1 now
where the time goes in v5:
time: 65.2 us; the launch traced here: 65 us
  Pallas kernels  62.2 us (95%)
  local copies, waits for them, and re-layouts  2.18 us (3%)
    pallas_call x1, Pallas kernels, on_device(): pl.pallas_call(kernel, out_shape=(jax.ShapeDtypeStruct((2, 8, NC, HD), BF...  62.2 us
    unnamed x4, local copies, waits for them, and re-layouts  2.18 us

profile of v5, /device:TPU:1, one launch (start us, length us, event | category | flops | bytes accessed | tf_op | source)
XLA Modules:
  0.0 65.0 jit_solution(468576571634492829)
XLA Ops:
  0.6 62.2 %shard_map.104 = (bf16[2,8,32,128]{3,2,1,0:T(8,128)(2,1)}, f32[8,512]{1,0:T(8,128)}) custom-call(f32[8,512]{1,0:T(8,128)} %stream_h.1, s32[8,2,32]{2,1,0:T(2,128)} %ids_h.1, f32[1,512]{1,0:T(1,128)} %bitcast.11, bf16[512,1024]{1,0:T(8,128)(2,1)} %proj_h.1, bf16[32,64,256]{2,1,0:T(8,128)(2,1)} %bitcast.7, bf16[31,16,256]{2,1,0:T(8,128)(2,1)} %bitcast.10, ...), custom_call_target="tpu_custom_call" | custom-call | tf_op jit(solution)/shard_map/pallas_call | solution.py:421
  62.8 0.0 copy-start
  62.9 1.6 %copy.13 = bf16[2,8,32,128]{3,2,1,0:T(8,128)(2,1)} copy(bf16[2,8,32,128]{3,2,1,0:T(8,128)(2,1)} %get-tuple-element.4) | data formatting | bytes 262144
  64.4 0.0 copy-done
  64.4 0.6 copy.14
Async XLA Ops:
  62.8 1.6 %copy-start = (f32[8,512]{1,0:T(8,128)S(1)}, f32[8,512]{1,0:T(8,128)}, u32[]{:S(2)}) copy-start(f32[8,512]{1,0:T(8,128)} %get-tuple-element.5) | copy-start | bytes 49156

commit v6 on v5

--- a/solution.py
+++ b/solution.py
@@ -204,6 +204,10 @@
         else:
             remote(cb.at[to], cr.at[t], snd.at[10], rcv.at[10], b, to)
 
+    drain(code_v.at[pl.ds(0, 4)], rcv.at[5])
+    send_quarter(0, down // 2, wq, wo, snd.at[7], rcv.at[17], b, up)
+    drain(code_v.at[pl.ds(0, 4)], rcv.at[8])
+    send_quarter(1, up // 2, wq, wo, snd.at[7], rcv.at[17], b, down)
     drain(tb, rcv.at[3])
     here = g // 2 * 2 + z // 8
 
@@ -247,6 +251,10 @@
     lax.fori_loop(0, 4, depth_block, 0)
 
 
+    drain(code_v.at[pl.ds(0, 4)], rcv.at[6])
+    share_with_core(down // 2, rcv.at[19])
+    drain(code_v.at[pl.ds(0, 4)], rcv.at[7])
+    share_with_core(up // 2, rcv.at[20])
     drain(cr, rcv.at[10])
     sums = cr[0].astype(F32)
     for part in range(1, 8):
@@ -273,14 +281,9 @@
         def _(src=src, dst=dst, to_b=to_b):
             remote(src, dst, snd.at[12], rcv.at[12], to_b, owner_t)
 
-    drain(code_v.at[pl.ds(0, 4)], rcv.at[5])
-    send_quarter(0, down // 2, wq, wo, snd.at[7], rcv.at[17], b, up)
-    drain(code_v.at[pl.ds(0, 4)], rcv.at[8])
-    send_quarter(1, up // 2, wq, wo, snd.at[7], rcv.at[17], b, down)
-    drain(code_v.at[pl.ds(0, 4)], rcv.at[6])
-    share_with_core(down // 2, rcv.at[19])
-    drain(code_v.at[pl.ds(0, 4)], rcv.at[7])
-    share_with_core(up // 2, rcv.at[20])
+    drain(code_v.at[pl.ds(0, 8)], rcv.at[17])
+    share_with_core((head + 2) % 4, rcv.at[21])
+
 
     drain(rb, rcv.at[9])
     quarter = lane_iota((16, 128)) // 32
@@ -318,9 +321,6 @@
         if frame == 0:
             send_leading(1, stream_v[...])
     local(stream_v, next_o, loc.at[1])
-
-    drain(code_v.at[pl.ds(0, 8)], rcv.at[17])
-    share_with_core((head + 2) % 4, rcv.at[21])
 
     drain(xm, rcv.at[11])
     xa[...] = xm[...].astype(F32).reshape(1024, 128)

time: 65.2 us -> 64 us (0.982)
  Pallas kernels: 62.2 us -> 61.1 us
    pallas_call x1, Pallas kernels: 62.2 us -> 61.1 us  [on_device(): pl.pallas_call(kernel, out_shape=(jax.ShapeDtypeStruct((2, 8, NC, HD), BF...]
where the time goes in v6:
time: 64 us; the launch traced here: 63.9 us
  Pallas kernels  61.1 us (95%)
  local copies, waits for them, and re-layouts  2.18 us (3%)
  between operations  0.65 us (1%)
    pallas_call x1, Pallas kernels, on_device(): pl.pallas_call(kernel, out_shape=(jax.ShapeDtypeStruct((2, 8, NC, HD), BF...  61.1 us
    unnamed x4, local copies, waits for them, and re-layouts  2.18 us

profile of v6, /device:TPU:1, one launch (start us, length us, event | category | flops | bytes accessed | tf_op | source)
XLA Modules:
  0.0 63.9 jit_solution(8364815230052434720)
XLA Ops:
  0.6 61.1 %shard_map.104 = (bf16[2,8,32,128]{3,2,1,0:T(8,128)(2,1)}, f32[8,512]{1,0:T(8,128)}) custom-call(f32[8,512]{1,0:T(8,128)} %stream_h.1, s32[8,2,32]{2,1,0:T(2,128)} %ids_h.1, f32[1,512]{1,0:T(1,128)} %bitcast.11, bf16[512,1024]{1,0:T(8,128)(2,1)} %proj_h.1, bf16[32,64,256]{2,1,0:T(8,128)(2,1)} %bitcast.7, bf16[31,16,256]{2,1,0:T(8,128)(2,1)} %bitcast.10, ...), custom_call_target="tpu_custom_call" | custom-call | tf_op jit(solution)/shard_map/pallas_call | solution.py:421
  61.7 0.0 copy-start
  61.7 1.6 %copy.13 = bf16[2,8,32,128]{3,2,1,0:T(8,128)(2,1)} copy(bf16[2,8,32,128]{3,2,1,0:T(8,128)(2,1)} %get-tuple-element.4) | data formatting | bytes 262144
  63.3 0.0 copy-done
  63.3 0.6 copy.14
Async XLA Ops:
  61.7 1.6 %copy-start = (f32[8,512]{1,0:T(8,128)S(1)}, f32[8,512]{1,0:T(8,128)}, u32[]{:S(2)}) copy-start(f32[8,512]{1,0:T(8,128)} %get-tuple-element.5) | copy-start | bytes 49156

commit v7 on v6

--- a/solution.py
+++ b/solution.py
@@ -28,7 +28,7 @@
     stream_h, ids_h, bgain_h, proj_h, code_h, depth_h, dgain_h, qkv_h, wo_h,
     states_o, next_o,
     ids_v, stream_v, bgain_v, proj_v, code_v, dgain_v, wq, wo,
-    ids_all, e_ids, idt, tb, sb, rb, ms, mb, xm, xa, xs, nx, ls, lr,
+    z_ids, g_ids, idt, tb, sb, rb, ms, mb, xm, xa, xs, nx, ls, lr,
     cb, cr, cs_src, cs, ob, fr, so,
     loc, snd, rcv,
 ):
@@ -67,11 +67,10 @@
     def greet(to_b, to_t):
         pl.semaphore_signal(barrier, inc=1, device_id=(to_b, to_t), device_id_type=MESH)
 
-    def greet_batch(step, carry):
-        greet((b + step) % 64, t)
-        return carry
-
-    lax.fori_loop(1, 64, greet_batch, 0)
+    for step in range(1, 16):
+        greet((z + step) % 16 * 4 + g, t)
+    for step in range(1, 4):
+        greet(z * 4 + (g + step) % 4, t)
     for step in range(1, 8):
         for side in range(2):
             greet(chip * 2 + side, (t + step) % 8)
@@ -85,17 +84,13 @@
     wo_copy = local(wo_h, wo.at[own_lanes, :], loc.at[7])
 
     ids_copy.wait()
-    slot = g * 16 + z
-    packed = ids_v[:, 0, :] * 2048 + ids_v[:, 1, :]
-    ids_all[slot] = jnp.concatenate([packed[r : r + 1, :] for r in range(8)], axis=1)
-
-    pl.semaphore_wait(barrier, 77)
-
-    def send_ids(step, carry):
-        remote(ids_all.at[slot], ids_all.at[slot], snd.at[0], rcv.at[0], (b + step) % 64, t)
-        return carry
-
-    lax.fori_loop(1, 64, send_ids, 0)
+    z_ids[z] = jnp.zeros((8, 128), F32)
+    z_ids[z, :, 0:NC] = (ids_v[:, 0, :] * 2048 + ids_v[:, 1, :]).astype(F32)
+
+    pl.semaphore_wait(barrier, 32)
+
+    for step in range(1, 16):
+        remote(z_ids.at[z], z_ids.at[z], snd.at[0], rcv.at[0], (z + step) % 16 * 4 + g, t)
     for step in range(16):
         to = (mine + step) % 16
         first = jnp.maximum(2 * to - 1, 0)
@@ -156,19 +151,15 @@
     proj_copy.wait()
     send_leading(0, stream_v[...])
 
-    drain(ids_all.at[pl.ds(0, 63)], rcv.at[0])
-
-    for gg in range(4):
-        for zh in range(2):
-            words = ids_all[pl.ds(gg * 16 + zh * 8, 8), 0, :]
-            for r in range(8):
-                half = words[:, r // 4 * 128 : r // 4 * 128 + 128]
-                if r % 4:
-                    half = pltpu.roll(half, 128 - 32 * (r % 4), 1)
-                e_ids[gg, pl.ds(zh * 64 + r, 8, stride=8), :] = half.astype(F32)
+    drain(z_ids.at[pl.ds(0, 15)], rcv.at[0])
+    g_ids[g] = jnp.transpose(z_ids[...].reshape(128, 128))[0:NC, :]
+    for step in range(1, 4):
+        remote(g_ids.at[g], g_ids.at[g], snd.at[2], rcv.at[2], z * 4 + (g + step) % 4, t)
+    drain(g_ids.at[pl.ds(0, 3)], rcv.at[2])
+
     first_half = lane_iota((NC, 128)) < 64
     for gg in range(4):
-        words = jnp.transpose(e_ids[gg])[0:NC, :].astype(jnp.int32)
+        words = g_ids[gg].astype(jnp.int32)
         early = (words >> 11).astype(F32)
         late = (words & 2047).astype(F32)
         block = gg // 2 * 4 + gg % 2
@@ -390,7 +381,8 @@
     drain(stream_v, loc.at[1])
     for frame in range(2):
         drain(so.at[frame], loc.at[2 + frame])
-    drain(ids_all.at[pl.ds(0, 63)], snd.at[0])
+    drain(z_ids.at[pl.ds(0, 15)], snd.at[0])
+    drain(g_ids.at[pl.ds(0, 3)], snd.at[2])
     drain(code_v.at[pl.ds(0, 15), pl.ds(0, 32), :], snd.at[3])
     drain(code_v.at[pl.ds(0, 16)], snd.at[4])
     for which in (5, 6, 7):
@@ -435,8 +427,8 @@
             vm((1, DD), F32),
             vm((3, DD, 4 * HD), BF16),
             vm((4 * HD, DD), BF16),
-            vm((64, 1, 256), jnp.int32),
-            vm((4, 128, 128), F32),
+            vm((16, 8, 128), F32),
+            vm((4, NC, 128), F32),
             vm((NC, 1024), F32),
             vm((2, 32, 2048), BF16),
             vm((32, 16, 128), BF16),

time: 64 us -> 59.7 us (0.933)
  Pallas kernels: 61.1 us -> 56.7 us
    pallas_call x1, Pallas kernels: 61.1 us -> 56.7 us  [on_device(): pl.pallas_call(kernel, out_shape=(jax.ShapeDtypeStruct((2, 8, NC, HD), BF...]
where the time goes in v7:
time: 59.7 us; the launch traced here: 59.5 us
  Pallas kernels  56.7 us (95%)
  local copies, waits for them, and re-layouts  2.18 us (4%)
  between operations  0.65 us (1%)
    pallas_call x1, Pallas kernels, on_device(): pl.pallas_call(kernel, out_shape=(jax.ShapeDtypeStruct((2, 8, NC, HD), BF...  56.7 us
    unnamed x4, local copies, waits for them, and re-layouts  2.18 us

profile of v7, /device:TPU:1, one launch (start us, length us, event | category | flops | bytes accessed | tf_op | source)
XLA Modules:
  0.0 59.5 jit_solution(6699448271043188404)
XLA Ops:
  0.6 56.7 %shard_map.104 = (bf16[2,8,32,128]{3,2,1,0:T(8,128)(2,1)}, f32[8,512]{1,0:T(8,128)}) custom-call(f32[8,512]{1,0:T(8,128)} %stream_h.1, s32[8,2,32]{2,1,0:T(2,128)} %ids_h.1, f32[1,512]{1,0:T(1,128)} %bitcast.11, bf16[512,1024]{1,0:T(8,128)(2,1)} %proj_h.1, bf16[32,64,256]{2,1,0:T(8,128)(2,1)} %bitcast.7, bf16[31,16,256]{2,1,0:T(8,128)(2,1)} %bitcast.10, ...), custom_call_target="tpu_custom_call" | custom-call | tf_op jit(solution)/shard_map/pallas_call | solution.py:413
  57.3 0.0 copy-start
  57.3 1.6 %copy.13 = bf16[2,8,32,128]{3,2,1,0:T(8,128)(2,1)} copy(bf16[2,8,32,128]{3,2,1,0:T(8,128)(2,1)} %get-tuple-element.4) | data formatting | bytes 262144
  58.9 0.0 copy-done
  58.9 0.6 %copy.14 = f32[8,512]{1,0:T(8,128)} copy(f32[8,512]{1,0:T(8,128)S(1)} %copy-done) | data formatting | bytes 32768
Async XLA Ops:
  57.3 1.6 %copy-start = (f32[8,512]{1,0:T(8,128)S(1)}, f32[8,512]{1,0:T(8,128)}, u32[]{:S(2)}) copy-start(f32[8,512]{1,0:T(8,128)} %get-tuple-element.5) | copy-start | bytes 49156
